TPU v7x, 512 devices: a whole 4x4x16 slice. The times are simulated.
512 devices in a mesh: gx: 4 (over y), gy: 8 (over x, core), gz: 16 (over z).
Axes of the slice: x: 4, y: 4, z: 16, core: 2. Of those that a mesh axis runs over, the one named last changes fastest.
Arguments:
- source: float32 [256, 256, 512], P('gz', 'gy', 'gx'), may hold values from -4 to 4
- labels: int32 [256, 256, 512], P('gz', 'gy', 'gx'), may hold values from 0 to 2
Outputs:
- potential: float32 [256, 256, 512], P('gz', 'gy', 'gx')
All inputs are finite; a program needn't handle non-finite values.
Results may differ from a plain program's by a relative error of at most 0.00002.
Values sent between devices are 32-bit elements; how exact they have to be, the bound alone decides.
A program may use at most 128 MiB of HBM per device.

v0:
```python
import jax
import jax.numpy as jnp
from jax import lax
from jax.sharding import PartitionSpec as P

LEVELS = 4
PRE = 2
POST = 2
COARSE = 6


SOLUTE_PERMITTIVITY = 0.1
SOLVENT_SCREENING = 0.004


def extended(block, sides, width):
    for axis, dim in sides:
        count = lax.axis_size(axis)
        forward = [(i, i + 1) for i in range(count - 1)]
        backward = [(target, source) for source, target in forward]
        low = lax.ppermute(
            lax.slice_in_dim(block, block.shape[dim] - width, None, axis=dim), axis, forward
        )
        high = lax.ppermute(lax.slice_in_dim(block, 0, width, axis=dim), axis, backward)
        block = jnp.concatenate([low, block, high], axis=dim)
    return block


def partner_2(x, axis, bit):
    return lax.ppermute(x, axis, [(i, i ^ 1 << bit) for i in range(lax.axis_size(axis))])


def neighbour_sum(padded):
    summed = padded[2:, 1:-1, 1:-1] + padded[:-2, 1:-1, 1:-1]
    summed = summed + padded[1:-1, 2:, 1:-1] + padded[1:-1, :-2, 1:-1]
    summed = summed + padded[1:-1, 1:-1, 2:] + padded[1:-1, 1:-1, :-2]
    return summed


def parity_grid(extent, offsets):
    total_index = offsets[0] + lax.broadcasted_iota(jnp.int32, extent, 0)
    total_index = total_index + offsets[1] + lax.broadcasted_iota(jnp.int32, extent, 1)
    total_index = total_index + offsets[2] + lax.broadcasted_iota(jnp.int32, extent, 2)
    return total_index % 2


def coarsen(field):
    depth_z, depth_y, depth_x = field.shape
    blocks = field.reshape(depth_z // 2, 2, depth_y // 2, 2, depth_x // 2, 2)
    return blocks.sum(axis=(1, 3, 5)) * 0.125


def refine(field):
    return jnp.repeat(jnp.repeat(jnp.repeat(field, 2, 0), 2, 1), 2, 2)


def local_smooth(field, right, weight, diagonal, parity, sweeps):
    for sweep in range(sweeps):
        for colour in (0, 1):
            summed = neighbour_sum(jnp.pad(field, 1))
            field = jnp.where(parity == colour, (right + weight * summed) / diagonal, field)
    return field


def local_cycle(grid_level, right, permittivity, screening):
    weight = permittivity * 0.25**grid_level
    diagonal = 6.0 * weight + screening
    parity = parity_grid(right.shape, (0, 0, 0))
    field = jnp.zeros_like(right)
    if grid_level == LEVELS:
        return local_smooth(field, right, weight, diagonal, parity, COARSE)
    field = local_smooth(field, right, weight, diagonal, parity, PRE)
    residual = right - (diagonal * field - weight * neighbour_sum(jnp.pad(field, 1)))
    correction = local_cycle(
        grid_level + 1, coarsen(residual), coarsen(permittivity), coarsen(screening)
    )
    field = field + refine(correction)
    return local_smooth(field, right, weight, diagonal, parity, POST)


def exchange_faces(field):
    return extended(field, (("gx", 2), ("gy", 1), ("gz", 0)), 1)


def shared_smooth(field, right, weight, diagonal, parity, sweeps, from_zero):
    for sweep in range(sweeps):
        for colour in (0, 1):
            if from_zero and sweep == 0 and (colour == 0):
                summed = jnp.zeros_like(field)
            else:
                summed = neighbour_sum(exchange_faces(field))
            field = jnp.where(parity == colour, (right + weight * summed) / diagonal, field)
    return field


def merge_partner(stacked, lower_half, partner, axis_number):
    joined_low = jnp.concatenate((stacked, partner), axis_number)
    joined_high = jnp.concatenate((partner, stacked), axis_number)
    return jnp.where(lower_half, joined_low, joined_high)


def merged_cycle(grid_level, right, permittivity, screening):
    extent = right.shape
    stacked = jnp.stack((right, permittivity, screening))
    for bit_number in range(lax.axis_size("gx").bit_length() - 1):
        partner = partner_2(stacked, "gx", bit_number)
        lower_half = (lax.axis_index("gx") >> bit_number) % 2 == 0
        stacked = merge_partner(stacked, lower_half, partner, 3)
    for bit_number in range(lax.axis_size("gy").bit_length() - 1):
        partner = partner_2(stacked, "gy", bit_number)
        lower_half = (lax.axis_index("gy") >> bit_number) % 2 == 0
        stacked = merge_partner(stacked, lower_half, partner, 2)
    for bit_number in range(lax.axis_size("gz").bit_length() - 1):
        partner = partner_2(stacked, "gz", bit_number)
        lower_half = (lax.axis_index("gz") >> bit_number) % 2 == 0
        stacked = merge_partner(stacked, lower_half, partner, 1)
    correction = local_cycle(grid_level, stacked[0], stacked[1], stacked[2])
    corner = (
        lax.axis_index("gz") * extent[0],
        lax.axis_index("gy") * extent[1],
        lax.axis_index("gx") * extent[2],
    )
    return lax.dynamic_slice(correction, corner, extent)


def shared_cycle(grid_level, right, permittivity, screening):
    weight = permittivity * 0.25**grid_level
    diagonal = 6.0 * weight + screening
    extent = right.shape
    offsets = (
        lax.axis_index("gz") * extent[0],
        lax.axis_index("gy") * extent[1],
        lax.axis_index("gx") * extent[2],
    )
    parity = parity_grid(extent, offsets)
    field = jnp.zeros_like(right)
    field = shared_smooth(field, right, weight, diagonal, parity, PRE, True)
    residual = right - (diagonal * field - weight * neighbour_sum(exchange_faces(field)))
    coarse_right = coarsen(residual)
    coarse_permittivity = coarsen(permittivity)
    coarse_screening = coarsen(screening)
    if grid_level + 1 == 3:
        correction = merged_cycle(
            grid_level + 1, coarse_right, coarse_permittivity, coarse_screening
        )
    else:
        correction = shared_cycle(
            grid_level + 1, coarse_right, coarse_permittivity, coarse_screening
        )
    field = field + refine(correction)
    return shared_smooth(field, right, weight, diagonal, parity, POST, False)


def local(source, labels):
    permittivity = jnp.where(labels == 1, SOLUTE_PERMITTIVITY, 1.0).astype(jnp.float32)
    screening = jnp.where(labels == 0, SOLVENT_SCREENING, 0.0).astype(jnp.float32)
    return shared_cycle(0, source, permittivity, screening)


def solution(mesh):
    return jax.shard_map(
        local,
        mesh=mesh,
        in_specs=(P("gz", "gy", "gx"), P("gz", "gy", "gx")),
        out_specs=P("gz", "gy", "gx"),
        check_vma=False,
    )
```

profile of v0, /device:TPU:1, one launch (start us, length us, event | category | flops | bytes accessed | tf_op | source)
XLA Modules:
  0.0 1068.0 jit_solution(12223540615298526599)
XLA Ops:
  39.6 9.1 fusion.7
  152.6 5.8 collective-permute-start.23
  160.0 18.1 %reshape.103 = f32[8,2,16,2,64,2]{5,4,3,2,1,0:T(8,128)} reshape(f32[16,32,128]{2,1,0:T(8,128)S(1)} %copy.593) | data formatting | bytes 524288 | tf_op jit(solution)/shard_map/reshape | solution.py:49
  179.7 18.1 %reshape.104 = f32[8,2,16,2,64,2]{5,4,3,2,1,0:T(8,128)} reshape(f32[16,32,128]{2,1,0:T(8,128)S(1)} %copy.594) | data formatting | bytes 524288 | tf_op jit(solution)/shard_map/reshape | solution.py:49
  197.7 7.0 reduce_sum.109
  204.7 7.0 reduce_sum.110
  211.8 8.3 fusion.15
  221.7 18.1 %reshape.102 = f32[8,2,16,2,64,2]{5,4,3,2,1,0:T(8,128)} reshape(f32[16,32,128]{2,1,0:T(8,128)S(1)} %copy.592) | data formatting | bytes 524288 | tf_op jit(solution)/shard_map/reshape | solution.py:49
  239.7 7.0 reduce_sum.108
  287.9 6.0 collective-permute-start.35
  312.4 5.9 collective-permute-start.41
  374.8 5.8 collective-permute-start.53
  398.3 5.8 collective-permute-start.59
  421.8 5.8 collective-permute-start.65
  485.2 8.1 collective-permute-start.78
  493.3 6.2 collective-permute-done.78
  499.5 8.7 collective-permute-start.79
  508.2 34.0 %collective-permute-done.79 = f32[3,8,32,64]{3,2,1,0:T(8,128)} collective-permute-done((f32[3,8,32,64]{3,2,1,0:T(8,128)S(1)}, f32[3,8,32,64]{3,2,1,0:T(8,128)}, u32[]{:S(2)}, u32[]{:S(2)}) %collective-permute-start.79) | collective-permute-done | bytes 196640 | tf_op jit(solution)/shard_map/ppermute | solution.py:30
  543.7 30.8 %collective-permute-start.80 = (f32[3,16,32,64]{3,2,1,0:T(8,128)S(1)}, f32[3,16,32,64]{3,2,1,0:T(8,128)}, u32[]{:S(2)}, u32[]{:S(2)}) collective-permute-start(f32[3,16,32,64]{3,2,1,0:T(8,128)S(1)} %maximum_select_fusion.1), channel_id=1, source_target_pairs={{0,8},{1,9},{2,10},{3,11},{4,12},{5,13},{6,14},{7,15},{8,0},{9,1},... | collective-permute-start | bytes 1179656 | tf_op jit(solution)/shard_map/ppermute | solution.py:30
  575.4 38.8 %collective-permute-done.80 = f32[3,16,32,64]{3,2,1,0:T(8,128)} collective-permute-done((f32[3,16,32,64]{3,2,1,0:T(8,128)S(1)}, f32[3,16,32,64]{3,2,1,0:T(8,128)}, u32[]{:S(2)}, u32[]{:S(2)}) %collective-permute-start.80) | collective-permute-done | bytes 393248 | tf_op jit(solution)/shard_map/ppermute | solution.py:30
  621.0 19.5 %reshape.107 = f32[16,2,16,2,32,2]{5,4,3,2,1,0:T(8,128)} reshape(f32[32,32,64]{2,1,0:T(8,128)} %fusion.105) | data formatting | bytes 524288 | tf_op jit(solution)/shard_map/reshape | solution.py:49
  640.4 7.1 reduce_sum.117
  647.6 19.5 %reshape_squeeze.6 = f32[16,2,16,2,32,2]{5,4,3,2,1,0:T(8,128)} reshape(f32[1,32,32,64]{3,2,1,0:T(8,128)} %get-tuple-element.25) | data formatting | bytes 524288 | tf_op jit(solution)/shard_map/reshape;squeeze | solution.py:49
  667.0 7.1 reduce_sum.118
  674.2 19.8 %reshape_squeeze.7 = f32[16,2,16,2,32,2]{5,4,3,2,1,0:T(8,128)} reshape(f32[1,32,32,64]{3,2,1,0:T(8,128)} %get-tuple-element.24) | data formatting | bytes 524288 | tf_op jit(solution)/shard_map/reshape;squeeze | solution.py:49
  694.0 7.1 reduce_sum.119
  720.4 14.1 %collective-permute-start.83 = (f32[4,1,34]{2,1,0:T(1,128)S(1)}, f32[4,1,34]{2,1,0:T(1,128)S(1)}, u32[]{:S(2)}, u32[]{:S(2)}) collective-permute-start(f32[4,1,34]{2,1,0:T(1,128)S(1)} %get-tuple-element.139), channel_id=1, source_target_pairs={{0,16},{16,32},{32,48},{48,64},{64,80},{80,96},{96,112},{1,17},{17... | collective-permute-start | bytes 1640 | tf_op jit(solution)/shard_map/ppermute | solution.py:21
  937.2 5.8 collective-permute-start.134
  976.0 6.0 collective-permute-start.140
  1013.3 5.8 collective-permute-start.146
  1052.1 5.8 collective-permute-start.152
  1059.2 6.1 fusion.27
  (573 shorter events, 687.2 us)
Async XLA Ops:
  16.2 10.4 collective-permute-start.2
  59.4 8.7 collective-permute-start.8
  98.5 7.3 collective-permute-start.14
  135.2 8.5 collective-permute-start.20
  151.3 60.4 %collective-permute-start.22 = (f32[1,34,130]{1,0,2:T(1,128)}, f32[1,34,130]{1,0,2:T(1,128)S(1)}, u32[]{:S(2)}, u32[]{:S(2)}) collective-permute-start(f32[1,34,130]{1,0,2:T(1,128)} %get-tuple-element.15), channel_id=1, source_target_pairs={{1,0},{2,1},{3,2},{4,3},{5,4},{6,5},{7,6},{8,7},{9,8},{10,9},{11,1... | collective-permute-start | bytes 53048 | tf_op jit(solution)/shard_map/ppermute | solution.py:24
  152.6 59.2 %collective-permute-start.23 = (f32[1,34,130]{1,0,2:T(1,128)}, f32[1,34,130]{1,0,2:T(1,128)}, u32[]{:S(2)}, u32[]{:S(2)}) collective-permute-start(f32[1,34,130]{1,0,2:T(1,128)} %get-tuple-element.16), channel_id=1, source_target_pairs={{0,1},{1,2},{2,3},{3,4},{4,5},{5,6},{6,7},{7,8},{8,9},{9,10},{10,1... | collective-permute-start | bytes 53048 | tf_op jit(solution)/shard_map/ppermute | solution.py:21
  286.6 7.3 collective-permute-start.34
  287.9 6.8 collective-permute-start.35
  311.1 7.2 collective-permute-start.40
  335.4 17.4 %collective-permute-start.46 = (f32[1,18,66]{2,1,0:T(8,128)S(1)}, f32[1,18,66]{2,1,0:T(8,128)S(1)}, u32[]{:S(2)}, u32[]{:S(2)}) collective-permute-start(f32[1,18,66]{2,1,0:T(8,128)S(1)} %get-tuple-element.73), channel_id=1, source_target_pairs={{1,0},{2,1},{3,2},{4,3},{5,4},{6,5},{7,6},{8,7},{9,8},{10,9},{11,1... | collective-permute-start | bytes 14264 | tf_op jit(solution)/shard_map/ppermute | solution.py:24
  336.7 16.2 %collective-permute-start.47 = (f32[1,18,66]{2,1,0:T(8,128)S(1)}, f32[1,18,66]{2,1,0:T(8,128)S(1)}, u32[]{:S(2)}, u32[]{:S(2)}) collective-permute-start(f32[1,18,66]{2,1,0:T(8,128)S(1)} %get-tuple-element.74), channel_id=1, source_target_pairs={{0,1},{1,2},{2,3},{3,4},{4,5},{5,6},{6,7},{7,8},{8,9},{9,10},{10,1... | collective-permute-start | bytes 14264 | tf_op jit(solution)/shard_map/ppermute | solution.py:21
  373.5 7.1 collective-permute-start.52
  397.0 7.1 collective-permute-start.58
  420.5 7.1 collective-permute-start.64
  478.1 7.1 collective-permute-start.77
  485.2 14.2 %collective-permute-start.78 = (f32[3,4,32,64]{3,2,1,0:T(8,128)S(1)}, f32[3,4,32,64]{3,2,1,0:T(8,128)S(1)}, u32[]{:S(2)}, u32[]{:S(2)}) collective-permute-start(f32[3,4,32,64]{3,2,1,0:T(8,128)S(1)} %maximum_select_fusion.3), channel_id=1, source_target_pairs={{0,2},{1,3},{2,0},{3,1},{4,6},{5,7},{6,4},{7,5},{8,10},{9,11},{10,... | collective-permute-start | bytes 294920 | tf_op jit(solution)/shard_map/ppermute | solution.py:30
  499.5 42.7 %collective-permute-start.79 = (f32[3,8,32,64]{3,2,1,0:T(8,128)S(1)}, f32[3,8,32,64]{3,2,1,0:T(8,128)}, u32[]{:S(2)}, u32[]{:S(2)}) collective-permute-start(f32[3,8,32,64]{3,2,1,0:T(8,128)S(1)} %maximum_select_fusion.2), channel_id=1, source_target_pairs={{0,4},{1,5},{2,6},{3,7},{4,0},{5,1},{6,2},{7,3},{8,12},{9,13},{10,... | collective-permute-start | bytes 589832 | tf_op jit(solution)/shard_map/ppermute | solution.py:30
  543.7 70.4 %collective-permute-start.80 = (f32[3,16,32,64]{3,2,1,0:T(8,128)S(1)}, f32[3,16,32,64]{3,2,1,0:T(8,128)}, u32[]{:S(2)}, u32[]{:S(2)}) collective-permute-start(f32[3,16,32,64]{3,2,1,0:T(8,128)S(1)} %maximum_select_fusion.1), channel_id=1, source_target_pairs={{0,8},{1,9},{2,10},{3,11},{4,12},{5,13},{6,14},{7,15},{8,0},{9,1},... | collective-permute-start | bytes 1179656 | tf_op jit(solution)/shard_map/ppermute | solution.py:30
  720.4 16.0 %collective-permute-start.83 = (f32[4,1,34]{2,1,0:T(1,128)S(1)}, f32[4,1,34]{2,1,0:T(1,128)S(1)}, u32[]{:S(2)}, u32[]{:S(2)}) collective-permute-start(f32[4,1,34]{2,1,0:T(1,128)S(1)} %get-tuple-element.139), channel_id=1, source_target_pairs={{0,16},{16,32},{32,48},{48,64},{64,80},{80,96},{96,112},{1,17},{17... | collective-permute-start | bytes 1640 | tf_op jit(solution)/shard_map/ppermute | solution.py:21
  901.8 7.2 collective-permute-start.127
  921.9 6.9 collective-permute-start.131
  935.9 7.1 collective-permute-start.133
  937.2 7.1 collective-permute-start.134
  959.3 8.3 collective-permute-start.137
  974.7 7.3 collective-permute-start.139
  976.0 7.1 collective-permute-start.140
  997.7 7.2 collective-permute-start.143
  1012.0 7.1 collective-permute-start.145
  1013.3 7.1 collective-permute-start.146
  1035.4 8.5 collective-permute-start.149
  1050.8 7.1 collective-permute-start.151
  1052.1 7.1 collective-permute-start.152
  (153 other events, 964.9 us)
where the time goes:
time: 1090 us; the launch traced here: 1070 us
  starting transfers between devices  463 us (42%)
  waiting for transfers between devices  251 us (23%)
  local copies, waits for them, and re-layouts  208 us (19%)
  other arithmetic  142 us (13%)
    ppermute x72, starting transfers between devices, extended(): lax.ppermute(lax.slice_in_dim(block, block.shape[dim] - width, None, axis...  285 us
    ppermute x72, waiting for transfers between devices, extended(): lax.ppermute(lax.slice_in_dim(block, 0, width, axis=dim), axis, backward)  137 us
    ppermute x72, starting transfers between devices, extended(): lax.ppermute(lax.slice_in_dim(block, 0, width, axis=dim), axis, backward)  111 us
    ppermute x9, waiting for transfers between devices, partner_2(): lax.ppermute(x, axis, [(i, i ^ 1 << bit) for i in range(lax.axis_size(axi...  91.6 us
    reshape x6, local copies, waits for them, and re-layouts, coarsen(): blocks = field.reshape(depth_z // 2, 2, depth_y // 2, 2, depth_x // 2, 2)  77.3 us
    ppermute x9, starting transfers between devices, partner_2(): lax.ppermute(x, axis, [(i, i ^ 1 << bit) for i in range(lax.axis_size(axi...  67.8 us
    reduce_sum x12, other arithmetic, coarsen(): return blocks.sum(axis=(1, 3, 5)) * 0.125  48.1 us
    select_n x21, other arithmetic, shared_smooth(): jnp.where(parity == colour, (right + weight * summed) / diagonal, field)  44.4 us
  transfers between devices with their start and end apart: 153, of which 85 were waited for; matrix products, arithmetic and copies ran while one was open for 8% of the time, Pallas kernels for 0%

commit v1 on v0

v1 whole, which is shorter than its diff:
```python
import functools

import jax
import jax.numpy as jnp
from jax import lax
from jax.experimental import pallas as pl
from jax.experimental.pallas import tpu as pltpu
from jax.sharding import PartitionSpec as P

COARSE = 6
SOLUTE_PERMITTIVITY = 0.1
SOLVENT_SCREENING = 0.004

MESH = pl.DeviceIdType.MESH
HIGHEST = lax.Precision.HIGHEST
F32 = jnp.float32
COPIES = 176

NZ, NY, NX = 16, 32, 128


def iota(shape, dim):
    return lax.broadcasted_iota(jnp.int32, shape, dim)


def tiled(tile, rows, lanes):
    tile = jnp.concatenate([tile] * (rows // 8), axis=0)
    return jnp.concatenate([tile] * (lanes // 128), axis=1)


def dot(a, b):
    return jnp.dot(a, b, precision=HIGHEST, preferred_element_type=F32)


def neighbours(v, p, edges):
    c = v[p]
    rows, lanes = c.shape
    below, above, left, right = edges
    s = v[p - 1] + v[p + 1]
    shifted = pltpu.roll(c, 1, 0)
    s = s + (shifted if below is None else jnp.where(below, 0.0, shifted))
    shifted = pltpu.roll(c, rows - 1, 0)
    s = s + (shifted if above is None else jnp.where(above, 0.0, shifted))
    shifted = pltpu.roll(c, 1, 1)
    s = s + (shifted if left is None else jnp.where(left, 0.0, shifted))
    shifted = pltpu.roll(c, lanes - 1, 1)
    s = s + (shifted if right is None else jnp.where(right, 0.0, shifted))
    return c, s


def parity_of(rows, lanes):
    return tiled((iota((8, 128), 0) + iota((8, 128), 1)) & 1, rows, lanes)


def pairs(start, stop, body):
    def step(i, carry):
        p = start + 2 * i
        body(p, start & 1)
        body(p + 1, (start + 1) & 1)
        return carry

    lax.fori_loop(0, (stop - start) // 2, step, 0)


def half_sweep(v, bd, wd, start, stop, colour, edges, shift=0):
    par = parity_of(*v.shape[1:])

    def body(p, odd):
        c, s = neighbours(v, p, edges)
        new = bd(p - shift) + wd(p - shift) * s
        v[p] = jnp.where(par == ((odd + colour + shift) & 1), new, c)

    pairs(start, stop, body)


def first_half(v, bd, start, stop, shift=0):
    par = parity_of(*v.shape[1:])

    def body(p, odd):
        v[p] = jnp.where(par == ((odd + shift) & 1), bd(p - shift), 0.0)

    pairs(start, stop, body)


def kernel(sizes, *refs):
    (source, labels, out, bdw0, v0, vp0, d0, tt, ee, tv, ev, sy, syv, sxm, sxc, sxmv, sxcv, pk, pkc, g1, g1c,
     c1, r1, v1, vp1, bd1, wd1, in1, c2, r2, v2, vp2, bd2, wd2, in2, z3, z3c, y3s, y3cs, y3, y3c, p3, p3c,
     c3, v3, bd3, wd3, in3, c4, v4, bd4, wd4, in4, work, work2, ssem, rsem) = refs
    count = dict(gx=sizes[0], gy=sizes[1], gz=sizes[2])
    gx, gy, gz = lax.axis_index("gx"), lax.axis_index("gy"), lax.axis_index("gz")
    number = [0]

    def device(offset):
        return tuple(
            lax.rem(here + (step + size) % size, size)
            for here, step, size in zip((gx, gy, gz), offset, sizes)
        )

    def send(source_ref, target_ref, offset):
        i = number[0]
        number[0] += 1
        copy = pltpu.make_async_remote_copy(
            src_ref=source_ref,
            dst_ref=target_ref,
            send_sem=ssem.at[i],
            recv_sem=rsem.at[i],
            device_id=device(offset),
            device_id_type=MESH,
        )
        copy.start()
        return copy

    def finish(copies):
        for copy in copies:
            copy.wait()

    peers = set()
    for a in (-1, 0, 1):
        for b in (-1, 0, 1):
            for c in (-1, 0, 1):
                peers.add((a, b, c))
    for b in (-1, 0, 1):
        for c in (-2, 2):
            peers.add((0, b, c))
    for i in range(1, sizes[0]):
        peers.add((i, 0, 0))
    for i in range(1, sizes[1]):
        peers.add((0, i, 0))
    for i in range(1, sizes[2]):
        peers.add((0, 0, i))
    peers = sorted({tuple(step % size for step, size in zip(o, sizes)) for o in peers} - {(0, 0, 0)})
    barrier = pltpu.get_barrier_semaphore()
    for offset in peers:
        pl.semaphore_signal(barrier, inc=1, device_id=device(offset), device_id_type=MESH)

    lane = iota((8, 128), 1)
    sub = iota((8, 128), 0)
    low4 = sub < 4
    x_lo, x_hi = gx > 0, gx < sizes[0] - 1
    y_lo, y_hi = gy > 0, gy < sizes[1] - 1
    z_lo, z_hi = gz > 0, gz < sizes[2] - 1

    ee[...] = jnp.zeros(ee.shape, F32)

    def prepare(z, carry):
        label = labels[z]
        permittivity = jnp.where(label == 1, SOLUTE_PERMITTIVITY, 1.0).astype(F32)
        screening = jnp.where(label == 0, SOLVENT_SCREENING, 0.0).astype(F32)
        diagonal = 6.0 * permittivity + screening
        inverse = 1.0 / diagonal
        d0[z] = diagonal
        for f, value in enumerate((source[z] * inverse, permittivity * inverse)):
            bdw0[f, z + 4, 0:NY, 0:NX] = value
            pack_edges(value, tt, ee, f, z)
        return carry

    def pack_edges(value, t_ref, e_ref, f, z):
        t_ref[f, z] = jnp.where(low4, value[0:8], value[NY - 8 : NY])
        group = tiled(lane >> 3, NY, 128)
        rolled = pltpu.roll(value, 8 * z + 4, 1)
        e_ref[f, 0:NY] = jnp.where(group == z, rolled, e_ref[f, 0:NY])

    def pack_corner(e_ref, f):
        e_ref[f, NY : NY + 8] = jnp.where(low4, e_ref[f, 0:8], e_ref[f, NY - 8 : NY])

    lax.fori_loop(0, NZ, prepare, 0)
    for f in (0, 1):
        pack_corner(ee, f)

    def slot(step):
        return 1 - step

    def send_halo0(own, target, t_ref, e_ref, y_ref, xm_ref, xc_ref):
        copies = []
        for c in (1, -1):
            first = 16 if c == 1 else 4
            copies.append(
                send(
                    own.at[:, pl.ds(first, 4), pl.ds(0, NY), pl.ds(0, NX)],
                    target.at[:, pl.ds(0 if c == 1 else 20, 4), pl.ds(0, NY), pl.ds(0, NX)],
                    (0, 0, c),
                )
            )
        for b in (1, -1):
            side = 0 if b == 1 else 1
            for c in (0, 1, -1):
                first, size, to = {0: (0, 16, 4), 1: (12, 4, 0), -1: (0, 4, 20)}[c]
                copies.append(
                    send(t_ref.at[:, pl.ds(first, size)], y_ref.at[side, :, pl.ds(to, size)], (0, b, c))
                )
        for a in (1, -1):
            side = 0 if a == 1 else 1
            for c in (0, 1, -1):
                copies.append(send(e_ref.at[:, pl.ds(0, NY)], xm_ref.at[side, slot(c)], (a, 0, c)))
                for b in (1, -1):
                    copies.append(
                        send(
                            e_ref.at[:, pl.ds(NY, 8)],
                            xc_ref.at[side, slot(c), 0 if b == 1 else 1],
                            (a, b, c),
                        )
                    )
        return copies

    in_low_half = (lane & 7) >= 4

    def fill_halo0(target, f, y_ref, xm_ref, xc_ref):
        x_valid = jnp.where(in_low_half, x_hi.astype(jnp.int32), x_lo.astype(jnp.int32))
        y_valid = jnp.where(low4, y_hi.astype(jnp.int32), y_lo.astype(jnp.int32))
        xy_valid = x_valid * y_valid
        edge_lanes = ((lane < 4) | (lane >= 124)).astype(jnp.int32)
        lane_main = tiled(in_low_half.astype(jnp.int32), NY, 128) > 0
        valid_main = tiled(x_valid, NY, 128) > 0
        edges = tiled(edge_lanes, NY + 8, 128)
        for part, (first, size, z_first, z_valid) in enumerate(
            ((0, 4, 12, z_lo), (4, 16, 0, None), (20, 4, 0, z_hi))
        ):
            ok = jnp.int32(1) if z_valid is None else z_valid.astype(jnp.int32)
            main = jnp.where(lane_main, xm_ref[1, part, f], xm_ref[0, part, f])
            main = jnp.where(valid_main, main, 0.0)
            below = jnp.where(in_low_half, xc_ref[1, part, 0, f], xc_ref[0, part, 0, f])
            above = jnp.where(in_low_half, xc_ref[1, part, 1, f], xc_ref[0, part, 1, f])
            corner = jnp.where(xy_valid > 0, jnp.where(low4, above, below), 0.0)
            packed = jnp.concatenate([main, corner], axis=0)

            def plane(i, carry):
                p = first + i
                rolled = pltpu.roll(packed, 252 - 8 * (z_first + i), 1)
                target[f, p, :, NX : 2 * NX] = jnp.where(edges * ok > 0, rolled, 0.0)
                rows = jnp.where(low4, y_ref[1, f, p], y_ref[0, f, p])
                target[f, p, NY : NY + 8, 0:NX] = jnp.where(y_valid * ok > 0, rows, 0.0)
                if z_valid is not None:
                    whole = target[f, p, 0:NY, 0:NX]
                    target[f, p, 0:NY, 0:NX] = jnp.where(tiled(0 * lane + ok, NY, NX) > 0, whole, 0.0)
                return carry

            lax.fori_loop(0, size, plane, 0)

    pl.semaphore_wait(barrier, len(peers))
    halo0 = send_halo0(bdw0, bdw0, tt, ee, sy, sxm, sxc)

    row_i, lane_i = iota((128, 128), 0), iota((128, 128), 1)
    to_low = jnp.where((row_i >> 1) == lane_i, 0.125, 0.0).astype(F32)
    to_high = jnp.where((row_i >> 1) == lane_i - 64, 0.125, 0.0).astype(F32)

    def rows_summed(size):
        half = size // 2
        return work[pl.ds(0, half, stride=2), :] + work[pl.ds(1, half, stride=2), :]

    def pack_level1(target, f):
        summed = rows_summed(256)
        target[f] = dot(summed[0:64], to_low) + dot(summed[64:128], to_high)

    def gather_gx(packed, slots):
        slots[gx] = packed[...]
        return [send(packed, slots.at[gx], (i, 0, 0)) for i in range(1, sizes[0])]

    def unpack_level1(slots, target, f):
        low = tiled((lane < 64).astype(jnp.int32), 16, 128) > 0
        for pair in range(2):
            for p in range(4):
                a = slots[2 * pair, f, pl.ds(16 * p, 16)]
                b = slots[2 * pair + 1, f, pl.ds(16 * p, 16)]
                lanes = slice(128 * pair, 128 * pair + 128)
                target(p, lanes, jnp.where(low, a, pltpu.roll(b, 64, 1)))
                target(p + 4, lanes, jnp.where(low, pltpu.roll(a, 64, 1), b))

    def coefficient(f, z):
        label = labels[z]
        if f == 0:
            return jnp.where(label == 1, SOLUTE_PERMITTIVITY, 1.0).astype(F32)
        return jnp.where(label == 0, SOLVENT_SCREENING, 0.0).astype(F32)

    for f in (0, 1):
        for k in range(8):
            work[32 * k : 32 * k + 32, :] = coefficient(f, 2 * k) + coefficient(f, 2 * k + 1)
        pack_level1(pkc, f)
    coef1 = gather_gx(pkc, g1c)

    finish(halo0)
    for f in (0, 1):
        fill_halo0(bdw0, f, sy, sxm, sxc)

    def send_halo1(own, target, width):
        copies = []
        for c in (0, 1, -1):
            planes = {0: (8, 8, 8), 1: (16 - width, width, 8 - width), -1: (8, width, 16)}[c]
            for b in (0, 1, -1):
                rows = {0: (0, 16, 0), 1: (8, 8, 24), -1: (0, 8, 16)}[b]
                if (b, c) != (0, 0):
                    copies.append(
                        send(
                            own(pl.ds(planes[0], planes[1]), pl.ds(rows[0], rows[1])),
                            target(pl.ds(planes[2], planes[1]), pl.ds(rows[2], rows[1])),
                            (0, b, c),
                        )
                    )
        return copies

    def send_halo2(own, target, steps):
        copies = []
        for c in steps:
            for b in (0, 1, -1):
                if (b, c) != (0, 0):
                    copies.append(
                        send(
                            own(pl.ds(8, 4), pl.ds(0, 8)),
                            target(pl.ds(8 - 4 * c, 4), pl.ds({0: 0, 1: 16, -1: 8}[b], 8)),
                            (0, b, c),
                        )
                    )
        return copies

    finish(coef1)
    for f in (0, 1):

        def put(p, lanes, value):
            c1[f, 8 + p, 0:16, lanes] = value

        unpack_level1(g1c, put, f)
    view1 = lambda a, b: c1.at[:, a, b]
    coef1 = send_halo1(view1, view1, 5)

    bd0_at = lambda p: bdw0[0, p]
    wd0_at = lambda p: bdw0[1, p]
    no_edges = (None,) * 4
    first_half(v0.at[0], bd0_at, 0, 24)
    half_sweep(v0.at[0], bd0_at, wd0_at, 1, 23, 1, no_edges)
    half_sweep(v0.at[0], bd0_at, wd0_at, 2, 22, 0, no_edges)
    half_sweep(v0.at[0], bd0_at, wd0_at, 3, 21, 1, no_edges)

    def residual0(k, carry):
        total = None
        for p in (4 + 2 * k, 5 + 2 * k):
            c, s = neighbours(v0.at[0], p, no_edges)
            value = bdw0[0, p, 0:NY, 0:NX] - c[0:NY, 0:NX] + bdw0[1, p, 0:NY, 0:NX] * s[0:NY, 0:NX]
            value = d0[p - 4] * value
            total = value if total is None else total + value
        work[pl.ds(pl.multiple_of(32 * k, 32), 32), :] = total
        return carry

    lax.fori_loop(0, 8, residual0, 0)
    pack_level1(pk, 0)
    right1 = gather_gx(pk, g1)

    ev[...] = jnp.zeros(ev.shape, F32)

    def pack_v(z, carry):
        value = v0[0, z + 4, 0:NY, 0:NX]
        pack_edges(value, tv, ev, 0, z)
        vp0[0, z + 4, 0:NY, 0:NX] = value
        return carry

    lax.fori_loop(0, NZ, pack_v, 0)
    pack_corner(ev, 0)
    halo_v0 = send_halo0(v0, vp0, tv, ev, syv, sxmv, sxcv)

    finish(coef1)

    def row_valid(rows, own):
        tiles = [jnp.ones((8, 128), jnp.int32)] * (own // 8)
        tiles += [0 * lane + y_hi.astype(jnp.int32), 0 * lane + y_lo.astype(jnp.int32)]
        return jnp.concatenate(tiles, axis=0)

    def plane_valid(p, below, size):
        before = jnp.where(p < below, z_lo.astype(jnp.int32), 1)
        behind = jnp.where(p >= below + size, z_hi.astype(jnp.int32), 1)
        return before * behind

    def coefficients(c_at, wd_at, in_at, planes, scale, valid):
        def body(p, carry):
            weight = c_at(0, p) * scale
            diagonal = 6.0 * weight + c_at(1, p)
            ok = diagonal > 0.0
            if valid is not None:
                ok = ok & (valid(p) > 0)
            inverse = jnp.where(ok, 1.0 / jnp.where(ok, diagonal, 1.0), 0.0)
            in_at[p] = inverse
            wd_at[p] = weight * inverse
            return carry

        lax.fori_loop(planes[0], planes[1], body, 0)

    rows1 = jnp.concatenate([row_valid(32, 16)] * 2, axis=1)
    rows2 = row_valid(24, 8)

    def valid1(p):
        return rows1 * plane_valid(p, 8, 8)

    def valid2(p):
        z = gz * 4 + p - 8
        ok = jnp.where(z >= 0, 1, 0) * jnp.where(z < 4 * sizes[2], 1, 0)
        return rows2 * ok

    coefficients(lambda f, p: c1[f, p], wd1, in1, (3, 21), 0.25, valid1)

    half_i, half_l = iota((256, 128), 0), iota((256, 128), 1)
    to_half = jnp.where((half_i >> 1) == half_l, 0.125, 0.0).astype(F32)

    def coarsen_level1(pair):
        for k in range(4):
            total = pair(k)
            for h in (0, 1):
                work2[h, 16 * k : 16 * k + 16, :] = total[:, 128 * h : 128 * h + 128]
        halves = [work2[h, pl.ds(0, 32, stride=2), :] + work2[h, pl.ds(1, 32, stride=2), :] for h in (0, 1)]
        return dot(jnp.concatenate(halves, axis=1), to_half)

    for f in (0, 1):
        coarse = coarsen_level1(lambda k: c1[f, 8 + 2 * k, 0:16] + c1[f, 9 + 2 * k, 0:16])
        for k in range(4):
            c2[f, 8 + k, 0:8] = coarse[8 * k : 8 * k + 8]
    view2 = lambda a, b: c2.at[:, a, b]
    coef2 = send_halo2(view2, view2, (0, 1, -1, 2, -2))

    finish(right1)

    def put_right(p, lanes, value):
        r1[8 + p, 0:16, lanes] = value

    unpack_level1(g1, put_right, 0)
    view_r1 = lambda a, b: r1.at[a, b]
    right1 = send_halo1(view_r1, view_r1, 5)

    finish(coef2)
    coefficients(lambda f, p: c2[f, p], wd2, in2, (2, 18), 0.0625, valid2)

    third_lane = lane_i - jnp.where(gz >= sizes[2] // 2, 64, 0)
    to_third = jnp.where(((row_i >> 1) == third_lane) & (third_lane >= 0) & (third_lane < 64), 0.125, 0.0)
    to_third = to_third.astype(F32)

    def coarsen_level2(pair):
        for k in range(2):
            work[8 * k : 8 * k + 8, :] = pair(k)
        return dot(rows_summed(16), to_third)

    def gather_gz(piece, slots):
        slots[gz] = piece[...]
        return [send(piece, slots.at[gz], (0, 0, i)) for i in range(1, sizes[2])]

    def gather_gy(slots, packed, target, fields):
        for f in range(fields):
            for k in range(8):
                packed[f, k] = slots[k, f] + slots[k + 8, f]
        target[gy] = packed[...]
        return [send(packed, target.at[gy], (0, i, 0)) for i in range(1, sizes[1])]

    for f in (0, 1):
        p3c[f] = coarsen_level2(lambda k: c2[f, 8 + 2 * k, 0:8] + c2[f, 9 + 2 * k, 0:8])
    coef3 = gather_gz(p3c, z3c)

    finish(halo_v0)
    fill_halo0(vp0, 0, syv, sxmv, sxcv)

    finish(right1)

    def scaled(target, right, inverse, start, stop):
        def body(p, carry):
            target[p] = right[p] * inverse[p]
            return carry

        lax.fori_loop(start, stop, body, 0)

    scaled(bd1, r1, in1, 3, 21)
    lanes1 = jnp.concatenate([lane, lane + 128], axis=1)
    lanes1 = jnp.concatenate([lanes1] * 4, axis=0)
    edges1 = (None, None, lanes1 == 0, lanes1 == 255)
    bd1_at = lambda p: bd1[p]
    wd1_at = lambda p: wd1[p]
    first_half(v1, bd1_at, 4, 20)
    half_sweep(v1, bd1_at, wd1_at, 5, 19, 1, edges1)
    half_sweep(v1, bd1_at, wd1_at, 6, 18, 0, edges1)
    half_sweep(v1, bd1_at, wd1_at, 7, 17, 1, edges1)

    def residual1(k):
        total = None
        for p in (8 + 2 * k, 9 + 2 * k):
            c, s = neighbours(v1, p, edges1)
            diagonal = 1.5 * c1[0, p, 0:16] + c1[1, p, 0:16]
            value = diagonal * (bd1[p, 0:16] - c[0:16] + wd1[p, 0:16] * s[0:16])
            total = value if total is None else total + value
        return total

    coarse = coarsen_level1(residual1)
    for k in range(4):
        r2[8 + k, 0:8] = coarse[8 * k : 8 * k + 8]
    view_r2 = lambda a, b: r2.at[a, b]
    right2 = send_halo2(view_r2, view_r2, (0, 1, -1))
    right2_far = send_halo2(view_r2, view_r2, (2, -2))
    for k in range(8):
        vp1[8 + k, 0:16] = v1[8 + k, 0:16]
    halo_v1 = send_halo1(lambda a, b: v1.at[a, b], lambda a, b: vp1.at[a, b], 6)
    finish(coef3)
    coef3 = gather_gy(z3c, y3cs, y3c, 2)

    finish(right2)
    scaled(bd2, r2, in2, 4, 16)
    lanes2 = jnp.concatenate([lane] * 3, axis=0)
    edges2 = (None, None, lanes2 == 0, lanes2 == 127)
    bd2_at = lambda p: bd2[p]
    wd2_at = lambda p: wd2[p]
    first_half(v2, bd2_at, 4, 16)
    half_sweep(v2, bd2_at, wd2_at, 5, 15, 1, edges2)
    half_sweep(v2, bd2_at, wd2_at, 6, 14, 0, edges2)
    half_sweep(v2, bd2_at, wd2_at, 7, 13, 1, edges2)

    def residual2(k):
        total = None
        for p in (8 + 2 * k, 9 + 2 * k):
            c, s = neighbours(v2, p, edges2)
            diagonal = 0.375 * c2[0, p, 0:8] + c2[1, p, 0:8]
            value = diagonal * (bd2[p, 0:8] - c[0:8] + wd2[p, 0:8] * s[0:8])
            total = value if total is None else total + value
        return total

    p3[0] = coarsen_level2(residual2)
    right3 = gather_gz(p3, z3)
    for k in range(4):
        vp2[8 + k, 0:8] = v2[8 + k, 0:8]
    halo_v2 = send_halo2(lambda a, b: v2.at[a, b], lambda a, b: vp2.at[a, b], (0, 1, -1, 2, -2))

    finish(coef3)

    def unpack_level3(slots, f, put):
        for k in range(8):
            for t in range(4):
                a, b = slots[2 * t, f, k], slots[2 * t + 1, f, k]
                put(2 * k, slice(8 * t, 8 * t + 8), jnp.where(low4, a, pltpu.roll(b, 4, 0)))
                put(2 * k + 1, slice(8 * t, 8 * t + 8), jnp.where(low4, pltpu.roll(a, 4, 0), b))

    for f in (0, 1):

        def put3(p, rows, value):
            c3[f, p, rows] = value

        unpack_level3(y3c, f, put3)
    coefficients(lambda f, p: c3[f, p], wd3, in3, (0, 16), 0.25**3, None)

    to_fourth = jnp.where(
        ((row_i >> 6) == (lane_i >> 6)) & (((row_i & 63) >> 1) == (lane_i & 63)), 0.125, 0.0
    ).astype(F32)

    def coarsen_level3(pair):
        for k in range(8):
            work[32 * k : 32 * k + 32, :] = pair(k)
        return dot(rows_summed(256), to_fourth)

    for f in (0, 1):
        coarse = coarsen_level3(lambda k: c3[f, 2 * k] + c3[f, 2 * k + 1])
        for k in range(8):
            c4[f, k] = coarse[16 * k : 16 * k + 16]
    coefficients(lambda f, p: c4[f, p], wd4, in4, (0, 8), 0.25**4, None)
    finish(right2_far)
    scaled(bd2, r2, in2, 2, 4)
    scaled(bd2, r2, in2, 16, 18)
    finish(halo_v1)

    def clean(target, valid, start, stop):
        def body(p, carry):
            target[p] = jnp.where(valid(p) > 0, target[p], 0.0)
            return carry

        lax.fori_loop(start, stop, body, 0)

    clean(vp1, valid1, 2, 22)

    finish(right3)
    right3 = gather_gy(z3, y3s, y3, 1)
    finish(halo_v2)
    clean(vp2, valid2, 0, 20)
    finish(right3)

    def put_bd3(p, rows, value):
        bd3[p, rows] = value * in3[p, rows]

    unpack_level3(y3, 0, put_bd3)

    def ends(v, planes):
        low = tiled((lane < 64).astype(jnp.int32), v.shape[1], 128) > 0
        v[0] = jnp.where(low, 0.0, pltpu.roll(v[planes], 64, 1))
        v[planes + 1] = jnp.where(low, pltpu.roll(v[1], 64, 1), 0.0)

    lanes3 = jnp.concatenate([lane & 63] * 4, axis=0)
    rows3 = iota((32, 128), 0)
    edges3 = (rows3 == 0, rows3 == 31, lanes3 == 0, lanes3 == 63)
    rows4 = iota((16, 128), 0)
    edges4 = (rows4 == 0, rows4 == 15, None, None)
    bd3_at = lambda p: bd3[p]
    wd3_at = lambda p: wd3[p]
    bd4_at = lambda p: bd4[p]
    wd4_at = lambda p: wd4[p]

    def half3(colour):
        ends(v3, 16)
        half_sweep(v3, bd3_at, wd3_at, 1, 17, colour, edges3, 1)

    def half4(colour):
        ends(v4, 8)
        half_sweep(v4, bd4_at, wd4_at, 1, 9, colour, edges4, 1)

    first_half(v3, bd3_at, 1, 17, 1)
    half3(1)
    half3(0)
    half3(1)
    ends(v3, 16)

    def residual3(k):
        total = None
        for p in (2 * k, 2 * k + 1):
            c, s = neighbours(v3, p + 1, edges3)
            diagonal = 6.0 * 0.25**3 * c3[0, p] + c3[1, p]
            value = diagonal * (bd3[p] - c + wd3[p] * s)
            total = value if total is None else total + value
        return total

    coarse = coarsen_level3(residual3)
    for k in range(8):
        bd4[k] = coarse[16 * k : 16 * k + 16] * in4[k]
    first_half(v4, bd4_at, 1, 9, 1)
    half4(1)

    def sweep4(i, carry):
        half4(0)
        half4(1)
        return carry

    lax.fori_loop(1, COARSE, sweep4, 0)

    from_fourth = jnp.where(
        ((row_i >> 6) == (lane_i >> 6)) & (((lane_i & 63) >> 1) == (row_i & 63)), 1.0, 0.0
    ).astype(F32)
    wide = jnp.concatenate([v4[1 + k] for k in range(8)], axis=0)
    wide = dot(wide, from_fourth)
    work[pl.ds(0, 128, stride=2), :] = wide
    work[pl.ds(1, 128, stride=2), :] = wide

    def add3(k, carry):
        correction = work[pl.ds(pl.multiple_of(32 * k, 32), 32), :]
        v3[1 + 2 * k] = v3[1 + 2 * k] + correction
        v3[2 + 2 * k] = v3[2 + 2 * k] + correction
        return carry

    lax.fori_loop(0, 8, add3, 0)
    half3(0)
    half3(1)
    half3(0)
    half3(1)

    from_third = jnp.where((lane_i >> 1) == (row_i & 63), 1.0, 0.0).astype(F32)
    lane_half = tiled(lane >> 6, 32, 128)
    picked = []
    for i in range(10):
        z = 2 * gz - 4 + i
        inside = jnp.where(z >= 0, 1, 0) * jnp.where(z < 32, 1, 0)
        z = jnp.clip(z, 0, 31)
        index, half = z & 15, z >> 4
        keep = jnp.where(lane_half == half, inside, 0) > 0
        picked.append(jnp.where(keep, v3[1 + index], 0.0))
    wide = dot(jnp.concatenate(picked, axis=0), from_third)
    work[pl.ds(0, 320, stride=2), :] = wide
    work[pl.ds(1, 320, stride=2), :] = wide
    own_row = pl.multiple_of(8 * gy, 8)
    next_row = pl.multiple_of(8 * jnp.minimum(gy + 1, sizes[1] - 1), 8)
    before_row = pl.multiple_of(8 * jnp.maximum(gy - 1, 0), 8)

    def add2(i, carry):
        base = pl.multiple_of(64 * i, 64)
        parts = [work[pl.ds(base + row, 8), :] for row in (own_row, next_row, before_row)]
        correction = jnp.where(rows2 > 0, jnp.concatenate(parts, axis=0), 0.0)
        vp2[2 * i] = vp2[2 * i] + correction
        vp2[2 * i + 1] = vp2[2 * i + 1] + correction
        return carry

    lax.fori_loop(0, 10, add2, 0)
    half_sweep(vp2, bd2_at, wd2_at, 2, 18, 0, edges2)
    half_sweep(vp2, bd2_at, wd2_at, 3, 17, 1, edges2)
    half_sweep(vp2, bd2_at, wd2_at, 4, 16, 0, edges2)
    half_sweep(vp2, bd2_at, wd2_at, 5, 15, 1, edges2)

    def spread(wide, rows):
        for h in (0, 1):
            part = wide[:, 128 * h : 128 * h + 128]
            work2[h, pl.ds(0, rows, stride=2), :] = part
            work2[h, pl.ds(1, rows, stride=2), :] = part

    def copied(base, rows):
        return jnp.concatenate([work2[h, pl.ds(base, rows), :] for h in (0, 1)], axis=1)

    wide_i, wide_l = iota((128, 256), 0), iota((128, 256), 1)
    from_second = jnp.where((wide_l >> 1) == wide_i, 1.0, 0.0).astype(F32)
    picked = []
    for p in range(5, 15):
        picked += [vp2[p, 0:8], jnp.where(low4, vp2[p, 8:16], vp2[p, 16:24])]
    wide = dot(jnp.concatenate(picked, axis=0), from_second)
    spread(wide, 160)

    def add1(i, carry):
        correction = copied(pl.multiple_of(32 * i, 32), 32)
        vp1[2 + 2 * i] = vp1[2 + 2 * i] + correction
        vp1[3 + 2 * i] = vp1[3 + 2 * i] + correction
        return carry

    lax.fori_loop(0, 10, add1, 0)
    half_sweep(vp1, bd1_at, wd1_at, 3, 21, 0, edges1)
    half_sweep(vp1, bd1_at, wd1_at, 4, 20, 1, edges1)
    half_sweep(vp1, bd1_at, wd1_at, 5, 19, 0, edges1)
    half_sweep(vp1, bd1_at, wd1_at, 6, 18, 1, edges1)

    first_i, first_l = iota((256, 256), 0), iota((256, 256), 1)
    column = jnp.where(first_l < NX + 4, first_l, jnp.where(first_l >= 2 * NX - 4, first_l - 2 * NX, -1024))
    from_first = jnp.where(((gx * NX + column) >> 1) == first_i, 1.0, 0.0).astype(F32)
    tile_low2 = jnp.concatenate([sub, sub], axis=1) < 2
    picked = []
    for p in range(6, 18):
        picked += [vp1[p, 0:16], jnp.where(tile_low2, vp1[p, 16:24], pltpu.roll(vp1[p, 24:32], 4, 0))]
    wide = dot(jnp.concatenate(picked, axis=0), from_first)
    spread(wide, 288)

    def add0(i, carry):
        correction = copied(pl.multiple_of(48 * i, 16), 40)
        vp0[0, 2 * i] = vp0[0, 2 * i] + correction
        vp0[0, 2 * i + 1] = vp0[0, 2 * i + 1] + correction
        return carry

    lax.fori_loop(0, 12, add0, 0)
    half_sweep(vp0.at[0], bd0_at, wd0_at, 1, 23, 0, no_edges)
    half_sweep(vp0.at[0], bd0_at, wd0_at, 2, 22, 1, no_edges)
    half_sweep(vp0.at[0], bd0_at, wd0_at, 3, 21, 0, no_edges)
    par = parity_of(NY, NX)

    def last(p, odd):
        c, s = neighbours(vp0.at[0], p, no_edges)
        new = bdw0[0, p, 0:NY, 0:NX] + bdw0[1, p, 0:NY, 0:NX] * s[0:NY, 0:NX]
        out[p - 4] = jnp.where(par == ((odd + 1) & 1), new, c[0:NY, 0:NX])

    pairs(4, 20, last)


def local(sizes, source, labels):
    vmem = lambda *shape: pltpu.VMEM(shape, F32)
    scratch = [
        vmem(2, 24, 40, 256),
        vmem(1, 24, 40, 256),
        vmem(1, 24, 40, 256),
        vmem(16, 32, 128),
        vmem(2, 16, 8, 128),
        vmem(2, 40, 128),
        vmem(1, 16, 8, 128),
        vmem(1, 40, 128),
        vmem(2, 2, 24, 8, 128),
        vmem(2, 1, 24, 8, 128),
        vmem(2, 3, 2, 32, 128),
        vmem(2, 3, 2, 2, 8, 128),
        vmem(2, 3, 1, 32, 128),
        vmem(2, 3, 2, 1, 8, 128),
        vmem(1, 64, 128),
        vmem(2, 64, 128),
        vmem(sizes[0], 1, 64, 128),
        vmem(sizes[0], 2, 64, 128),
        vmem(2, 24, 32, 256),
        vmem(24, 32, 256),
        vmem(24, 32, 256),
        vmem(24, 32, 256),
        vmem(24, 32, 256),
        vmem(24, 32, 256),
        vmem(24, 32, 256),
        vmem(2, 20, 24, 128),
        vmem(20, 24, 128),
        vmem(20, 24, 128),
        vmem(20, 24, 128),
        vmem(20, 24, 128),
        vmem(20, 24, 128),
        vmem(20, 24, 128),
        vmem(sizes[2], 1, 8, 128),
        vmem(sizes[2], 2, 8, 128),
        vmem(1, 8, 8, 128),
        vmem(2, 8, 8, 128),
        vmem(sizes[1], 1, 8, 8, 128),
        vmem(sizes[1], 2, 8, 8, 128),
        vmem(1, 8, 128),
        vmem(2, 8, 128),
        vmem(2, 16, 32, 128),
        vmem(18, 32, 128),
        vmem(16, 32, 128),
        vmem(16, 32, 128),
        vmem(16, 32, 128),
        vmem(2, 8, 16, 128),
        vmem(10, 16, 128),
        vmem(8, 16, 128),
        vmem(8, 16, 128),
        vmem(8, 16, 128),
        vmem(640, 128),
        vmem(2, 576, 128),
        pltpu.SemaphoreType.DMA((COPIES,)),
        pltpu.SemaphoreType.DMA((COPIES,)),
    ]
    return pl.pallas_call(
        functools.partial(kernel, sizes),
        out_shape=jax.ShapeDtypeStruct(source.shape, F32),
        in_specs=[pl.BlockSpec(memory_space=pltpu.VMEM)] * 2,
        out_specs=pl.BlockSpec(memory_space=pltpu.VMEM),
        scratch_shapes=scratch,
        compiler_params=pltpu.CompilerParams(
            collective_id=0, has_side_effects=True, vmem_limit_bytes=48 * 2**20
        ),
        name="v_cycle",
    )(source, labels)


def solution(mesh):
    sizes = tuple(mesh.shape[name] for name in ("gx", "gy", "gz"))
    return jax.shard_map(
        functools.partial(local, sizes),
        mesh=mesh,
        in_specs=(P("gz", "gy", "gx"), P("gz", "gy", "gx")),
        out_specs=P("gz", "gy", "gx"),
        check_vma=False,
    )
```

time: 1090 us -> 108 us (0.10); the launches traced: 1070 us -> 108 us
  starting transfers between devices: 463 us -> 0 us
  waiting for transfers between devices: 251 us -> 0 us
  local copies, waits for them, and re-layouts: 208 us -> 2.6 us
  other arithmetic: 142 us -> 0 us
  Pallas kernels: 0 us -> 105 us
    ppermute x153 -> x0, starting transfers between devices: 463 us -> none  [the longest x72 285 us: extended(): lax.ppermute(lax.slice_in_dim(block, block.shape[dim] - width, None, axis...]
    ppermute x153 -> x0, waiting for transfers between devices: 251 us -> none  [the longest x72 137 us: extended(): lax.ppermute(lax.slice_in_dim(block, 0, width, axis=dim), axis, backward)]
    pallas_call x0 -> x1, Pallas kernels: none -> 105 us  [local(): pl.pallas_call(functools.partial(kernel, sizes), out_shape=jax.ShapeDtype...]
    reshape x13 -> x0, local copies, waits for them, and re-layouts: 83 us -> none  [the longest x6 77.3 us: coarsen(): blocks = field.reshape(depth_z // 2, 2, depth_y // 2, 2, depth_x // 2, 2)]
    select_n x51 -> x0, other arithmetic: 56.4 us -> none  [the longest x21 44.4 us: shared_smooth(): jnp.where(parity == colour, (right + weight * summed) / diagonal, field)]
    reduce_sum x12 -> x0, other arithmetic: 48.1 us -> none  [coarsen(): return blocks.sum(axis=(1, 3, 5)) * 0.125]
    slice x48 -> x0, local copies, waits for them, and re-layouts: 39.8 us -> none  [the longest x40 25 us: extended(): lax.slice_in_dim(block, 0, width, axis=dim)]
    another operation x2 -> x0, local copies, waits for them, and re-layouts: 39.3 us -> none  [coarsen(): blocks = field.reshape(depth_z // 2, 2, depth_y // 2, 2, depth_x // 2, 2)]
  transfers between devices with their start and end apart: 153 -> 0, of which waited for: 85 -> 0; matrix products, arithmetic and copies ran while one was open for 8% -> 0% of each run, Pallas kernels for 0% -> 0%
where the time goes in v1:
time: 108 us
  Pallas kernels  105 us (97%)
  local copies, waits for them, and re-layouts  2.6 us (2%)
    pallas_call x1, Pallas kernels, local(): pl.pallas_call(functools.partial(kernel, sizes), out_shape=jax.ShapeDtype...  105 us
    unnamed x5, local copies, waits for them, and re-layouts  2.6 us

profile of v1, /device:TPU:1, one launch (start us, length us, event | category | flops | bytes accessed | tf_op | source)
XLA Modules:
  0.0 107.5 jit_solution(7045325001812467814)
XLA Ops:
  0.0 0.0 copy-start
  0.0 0.9 copy-done
  1.0 0.0 copy-start.1
  1.0 0.9 copy-done.1
  1.9 104.9 %v_cycle.1 = f32[16,32,128]{2,1,0:T(8,128)S(1)} custom-call(f32[16,32,128]{2,1,0:T(8,128)S(1)} %copy-done, s32[16,32,128]{2,1,0:T(8,128)S(1)} %copy-done.1), custom_call_target="tpu_custom_call" | custom-call | tf_op jit(solution)/shard_map/v_cycle/pallas_call | solution.py:796
  106.8 0.7 copy.4
Async XLA Ops:
  0.0 0.9 copy-start
  1.0 0.9 copy-start.1

commit v2 on v1

--- a/solution.py
+++ b/solution.py
@@ -2,6 +2,7 @@
 
 import jax
 import jax.numpy as jnp
+import numpy as np
 from jax import lax
 from jax.experimental import pallas as pl
 from jax.experimental.pallas import tpu as pltpu
@@ -16,6 +17,8 @@
 F32 = jnp.float32
 COPIES = 176
 
+B0, B1, B2 = 8, 10, 16
+
 NZ, NY, NX = 16, 32, 128
 
 
@@ -32,11 +35,10 @@
     return jnp.dot(a, b, precision=HIGHEST, preferred_element_type=F32)
 
 
-def neighbours(v, p, edges):
-    c = v[p]
+def neighbour_sum(before, c, behind, edges):
     rows, lanes = c.shape
     below, above, left, right = edges
-    s = v[p - 1] + v[p + 1]
+    s = before + behind
     shifted = pltpu.roll(c, 1, 0)
     s = s + (shifted if below is None else jnp.where(below, 0.0, shifted))
     shifted = pltpu.roll(c, rows - 1, 0)
@@ -45,47 +47,71 @@
     s = s + (shifted if left is None else jnp.where(left, 0.0, shifted))
     shifted = pltpu.roll(c, lanes - 1, 1)
     s = s + (shifted if right is None else jnp.where(right, 0.0, shifted))
-    return c, s
+    return s
+
+
+def neighbours(v, p, edges):
+    c = v[p]
+    return c, neighbour_sum(v[p - 1], c, v[p + 1], edges)
 
 
 def parity_of(rows, lanes):
     return tiled((iota((8, 128), 0) + iota((8, 128), 1)) & 1, rows, lanes)
 
 
-def pairs(start, stop, body):
+def far_first(size):
+    return sorted(range(1, size), key=lambda step: -min(step, size - step))
+
+
+def blocks(start, stop, block, body):
+    count = (stop - start) // block
+
     def step(i, carry):
-        p = start + 2 * i
-        body(p, start & 1)
-        body(p + 1, (start + 1) & 1)
+        body(start + block * i, start & 1, block)
         return carry
 
-    lax.fori_loop(0, (stop - start) // 2, step, 0)
-
-
-def half_sweep(v, bd, wd, start, stop, colour, edges, shift=0):
+    if count > 1:
+        lax.fori_loop(0, count, step, 0)
+    elif count == 1:
+        body(start, start & 1, block)
+    if start + count * block < stop:
+        first = start + count * block
+        body(first, first & 1, stop - first)
+
+
+def half_sweep(v, bd, wd, start, stop, colour, edges, block, shift=0):
     par = parity_of(*v.shape[1:])
 
-    def body(p, odd):
-        c, s = neighbours(v, p, edges)
-        new = bd(p - shift) + wd(p - shift) * s
-        v[p] = jnp.where(par == ((odd + colour + shift) & 1), new, c)
-
-    pairs(start, stop, body)
-
-
-def first_half(v, bd, start, stop, shift=0):
+    def body(first, odd, size):
+        before, c = v[first - 1], v[first]
+        for i in range(size):
+            p = first + i
+            behind = v[p + 1]
+            s = neighbour_sum(before, c, behind, edges)
+            new = bd(p - shift) + wd(p - shift) * s
+            v[p] = jnp.where(par == ((odd + i + colour + shift) & 1), new, c)
+            before, c = c, behind
+
+    blocks(start, stop, block, body)
+
+
+def first_half(v, bd, start, stop, block, shift=0):
     par = parity_of(*v.shape[1:])
 
-    def body(p, odd):
-        v[p] = jnp.where(par == ((odd + shift) & 1), bd(p - shift), 0.0)
-
-    pairs(start, stop, body)
+    def body(first, odd, size):
+        for i in range(size):
+            p = first + i
+            v[p] = jnp.where(par == ((odd + i + shift) & 1), bd(p - shift), 0.0)
+
+    blocks(start, stop, block, body)
 
 
 def kernel(sizes, *refs):
-    (source, labels, out, bdw0, v0, vp0, d0, tt, ee, tv, ev, sy, syv, sxm, sxc, sxmv, sxcv, pk, pkc, g1, g1c,
+    (source_hbm, labels_hbm, out, source, labels, isem, bdw0, v0, vp0, d0, tt, ee, tv, ev, sy, syv, sxm0, sxm1, sxm2, sxc0, sxc1, sxc2, *rest) = refs
+    (sxmv0, sxmv1, sxmv2, sxcv0, sxcv1, sxcv2, pk, pkc, g1, g1c,
      c1, r1, v1, vp1, bd1, wd1, in1, c2, r2, v2, vp2, bd2, wd2, in2, z3, z3c, y3s, y3cs, y3, y3c, p3, p3c,
-     c3, v3, bd3, wd3, in3, c4, v4, bd4, wd4, in4, work, work2, ssem, rsem) = refs
+     c3, v3, bd3, wd3, in3, c4, v4, bd4, wd4, in4, work, work2, ssem, rsem) = rest
+    sxmv, sxcv = (sxmv0, sxmv1, sxmv2), (sxcv0, sxcv1, sxcv2)
     count = dict(gx=sizes[0], gy=sizes[1], gz=sizes[2])
     gx, gy, gz = lax.axis_index("gx"), lax.axis_index("gy"), lax.axis_index("gz")
     number = [0]
@@ -133,6 +159,13 @@
     for offset in peers:
         pl.semaphore_signal(barrier, inc=1, device_id=device(offset), device_id_type=MESH)
 
+    loads = [
+        pltpu.make_async_copy(labels_hbm, labels, isem.at[0]),
+        pltpu.make_async_copy(source_hbm, source, isem.at[1]),
+    ]
+    for load in loads:
+        load.start()
+
     lane = iota((8, 128), 1)
     sub = iota((8, 128), 0)
     low4 = sub < 4
@@ -140,37 +173,43 @@
     y_lo, y_hi = gy > 0, gy < sizes[1] - 1
     z_lo, z_hi = gz > 0, gz < sizes[2] - 1
 
-    ee[...] = jnp.zeros(ee.shape, F32)
-
-    def prepare(z, carry):
-        label = labels[z]
-        permittivity = jnp.where(label == 1, SOLUTE_PERMITTIVITY, 1.0).astype(F32)
-        screening = jnp.where(label == 0, SOLVENT_SCREENING, 0.0).astype(F32)
-        diagonal = 6.0 * permittivity + screening
-        inverse = 1.0 / diagonal
+    def constants(label):
+        permittivity = np.array([1.0, SOLUTE_PERMITTIVITY, 1.0], np.float32)
+        screening = np.array([SOLVENT_SCREENING, 0.0, 0.0], np.float32)
+        diagonal = np.float32(6.0) * permittivity + screening
+        inverse = np.float32(1.0) / diagonal
+        choose = lambda t: jnp.where(label == 1, t[1], jnp.where(label == 0, t[0], t[2])).astype(F32)
+        return choose(inverse), choose(permittivity * inverse), choose(diagonal)
+
+    group = tiled(lane >> 3, NY, 128)
+
+    def gathered_edges(plane):
+        total = jnp.zeros((NY, 128), F32)
+        for z in range(NZ):
+            total = jnp.where(group == z, pltpu.roll(plane(z), 8 * z + 4, 1), total)
+        return jnp.concatenate([total, jnp.where(low4, total[0:8], total[NY - 8 : NY])], axis=0)
+
+    for load in loads:
+        load.wait()
+    for z in range(NZ):
+        inverse, relative, diagonal = constants(labels[z])
+        bd = source[z] * inverse
         d0[z] = diagonal
-        for f, value in enumerate((source[z] * inverse, permittivity * inverse)):
-            bdw0[f, z + 4, 0:NY, 0:NX] = value
-            pack_edges(value, tt, ee, f, z)
-        return carry
-
-    def pack_edges(value, t_ref, e_ref, f, z):
-        t_ref[f, z] = jnp.where(low4, value[0:8], value[NY - 8 : NY])
-        group = tiled(lane >> 3, NY, 128)
-        rolled = pltpu.roll(value, 8 * z + 4, 1)
-        e_ref[f, 0:NY] = jnp.where(group == z, rolled, e_ref[f, 0:NY])
-
-    def pack_corner(e_ref, f):
-        e_ref[f, NY : NY + 8] = jnp.where(low4, e_ref[f, 0:8], e_ref[f, NY - 8 : NY])
-
-    lax.fori_loop(0, NZ, prepare, 0)
-    for f in (0, 1):
-        pack_corner(ee, f)
+        bdw0[0, z + 4, 0:NY, 0:NX] = bd
+        bdw0[1, z + 4, 0:NY, 0:NX] = relative
+        tt[0, z] = jnp.where(low4, bd[0:8], pltpu.roll(relative[0:8], 4, 0))
+        tt[1, z] = jnp.where(low4, pltpu.roll(relative[NY - 8 : NY], 4, 0), bd[NY - 8 : NY])
+    edge_bd = gathered_edges(lambda z: bdw0[0, z + 4, 0:NY, 0:NX])
+    edge_wd = gathered_edges(lambda z: bdw0[1, z + 4, 0:NY, 0:NX])
+    ee[0], ee[1] = edge_bd, edge_wd
+    quarter = tiled(lane >> 5, NY + 8, 128)
+    inner = jnp.where(quarter == 1, pltpu.roll(edge_wd, 32, 1), pltpu.roll(edge_wd, 96, 1))
+    ee[2] = jnp.where((quarter == 0) | (quarter == 3), edge_bd, inner)
 
     def slot(step):
         return 1 - step
 
-    def send_halo0(own, target, t_ref, e_ref, y_ref, xm_ref, xc_ref):
+    def send_halo0(own, target, t_of, same_of, other_of, y_ref, xm_ref, xc_ref):
         copies = []
         for c in (1, -1):
             first = 16 if c == 1 else 4
@@ -181,63 +220,82 @@
                     (0, 0, c),
                 )
             )
-        for b in (1, -1):
-            side = 0 if b == 1 else 1
-            for c in (0, 1, -1):
-                first, size, to = {0: (0, 16, 4), 1: (12, 4, 0), -1: (0, 4, 20)}[c]
-                copies.append(
-                    send(t_ref.at[:, pl.ds(first, size)], y_ref.at[side, :, pl.ds(to, size)], (0, b, c))
-                )
-        for a in (1, -1):
-            side = 0 if a == 1 else 1
-            for c in (0, 1, -1):
-                copies.append(send(e_ref.at[:, pl.ds(0, NY)], xm_ref.at[side, slot(c)], (a, 0, c)))
+        for c in (1, -1, 0):
+            edges = other_of if c else same_of
+            to = slot(c)
+            for a in (1, -1):
+                side = 0 if a == 1 else 1
                 for b in (1, -1):
                     copies.append(
                         send(
-                            e_ref.at[:, pl.ds(NY, 8)],
-                            xc_ref.at[side, slot(c), 0 if b == 1 else 1],
+                            edges(pl.ds(NY, 8)),
+                            xc_ref[to].at[side, 0 if b == 1 else 1],
                             (a, b, c),
                         )
                     )
+            for b in (1, -1):
+                side = 0 if b == 1 else 1
+                first, size, start = {0: (0, 16, 4), 1: (12, 4, 0), -1: (0, 4, 20)}[c]
+                copies.append(send(t_of(b, pl.ds(first, size)), y_ref.at[side, pl.ds(start, size)], (0, b, c)))
+            for a in (1, -1):
+                side = 0 if a == 1 else 1
+                copies.append(send(edges(pl.ds(0, NY)), xm_ref[to].at[side], (a, 0, c)))
         return copies
 
     in_low_half = (lane & 7) >= 4
 
-    def fill_halo0(target, f, y_ref, xm_ref, xc_ref):
+    def fill_halo0(target, f, rows_of, columns, starts):
         x_valid = jnp.where(in_low_half, x_hi.astype(jnp.int32), x_lo.astype(jnp.int32))
         y_valid = jnp.where(low4, y_hi.astype(jnp.int32), y_lo.astype(jnp.int32))
         xy_valid = x_valid * y_valid
         edge_lanes = ((lane < 4) | (lane >= 124)).astype(jnp.int32)
         lane_main = tiled(in_low_half.astype(jnp.int32), NY, 128) > 0
-        valid_main = tiled(x_valid, NY, 128) > 0
-        edges = tiled(edge_lanes, NY + 8, 128)
-        for part, (first, size, z_first, z_valid) in enumerate(
-            ((0, 4, 12, z_lo), (4, 16, 0, None), (20, 4, 0, z_hi))
-        ):
+        for part, (first, size, z_valid) in enumerate(((0, 4, z_lo), (4, 16, None), (20, 4, z_hi))):
             ok = jnp.int32(1) if z_valid is None else z_valid.astype(jnp.int32)
-            main = jnp.where(lane_main, xm_ref[1, part, f], xm_ref[0, part, f])
-            main = jnp.where(valid_main, main, 0.0)
-            below = jnp.where(in_low_half, xc_ref[1, part, 0, f], xc_ref[0, part, 0, f])
-            above = jnp.where(in_low_half, xc_ref[1, part, 1, f], xc_ref[0, part, 1, f])
-            corner = jnp.where(xy_valid > 0, jnp.where(low4, above, below), 0.0)
+            (main_right, above_right, below_right), (main_left, above_left, below_left) = columns(part)
+            main = jnp.where(lane_main, main_right, main_left)
+            main = jnp.where(tiled(x_valid * ok, NY, 128) > 0, main, 0.0)
+            above = jnp.where(in_low_half, above_right, above_left)
+            below = jnp.where(in_low_half, below_right, below_left)
+            corner = jnp.where(xy_valid * ok > 0, jnp.where(low4, above, below), 0.0)
             packed = jnp.concatenate([main, corner], axis=0)
-
-            def plane(i, carry):
+            edges = tiled(edge_lanes, NY + 8, 128) > 0
+            row_ok = y_valid * ok > 0
+            for i in range(size):
                 p = first + i
-                rolled = pltpu.roll(packed, 252 - 8 * (z_first + i), 1)
-                target[f, p, :, NX : 2 * NX] = jnp.where(edges * ok > 0, rolled, 0.0)
-                rows = jnp.where(low4, y_ref[1, f, p], y_ref[0, f, p])
-                target[f, p, NY : NY + 8, 0:NX] = jnp.where(y_valid * ok > 0, rows, 0.0)
-                if z_valid is not None:
-                    whole = target[f, p, 0:NY, 0:NX]
-                    target[f, p, 0:NY, 0:NX] = jnp.where(tiled(0 * lane + ok, NY, NX) > 0, whole, 0.0)
-                return carry
-
-            lax.fori_loop(0, size, plane, 0)
-
-    pl.semaphore_wait(barrier, len(peers))
-    halo0 = send_halo0(bdw0, bdw0, tt, ee, sy, sxm, sxc)
+                rolled = pltpu.roll(packed, (252 - 8 * (starts[part] + i)) % 128, 1)
+                target[f, p, :, NX : 2 * NX] = jnp.where(edges, rolled, 0.0)
+                target[f, p, NY : NY + 8, 0:NX] = jnp.where(row_ok, rows_of(p), 0.0)
+            if z_valid is not None:
+
+                @pl.when(jnp.logical_not(z_valid))
+                def _():
+                    for i in range(size):
+                        target[f, first + i, 0:NY, 0:NX] = jnp.zeros((NY, NX), F32)
+
+    def fill_coefficients0():
+        for f in (0, 1):
+
+            def rows_of(p):
+                if f == 0:
+                    return jnp.where(low4, sy[1, p], sy[0, p])
+                return pltpu.roll(jnp.where(low4, sy[0, p], sy[1, p]), 4, 0)
+
+            def columns(part):
+                if part == 1:
+                    return [(sxm1[s, f], sxc1[s, 1, f], sxc1[s, 0, f]) for s in (1, 0)]
+                m, c = (sxm0, sxc0) if part == 0 else (sxm2, sxc2)
+                return [(m[s], c[s, 1], c[s, 0]) for s in (1, 0)]
+
+            fill_halo0(bdw0, f, rows_of, columns, ((12, 0, 0), (8, 0, 4))[f])
+
+    def fill_v0():
+        def columns(part):
+            m, c = sxmv[part], sxcv[part]
+            return [(m[s], c[s, 1], c[s, 0]) for s in (1, 0)]
+
+        fill_halo0(vp0, 0, lambda p: jnp.where(low4, syv[1, p], syv[0, p]), columns, (12, 0, 0))
+
 
     row_i, lane_i = iota((128, 128), 0), iota((128, 128), 1)
     to_low = jnp.where((row_i >> 1) == lane_i, 0.125, 0.0).astype(F32)
@@ -253,7 +311,7 @@
 
     def gather_gx(packed, slots):
         slots[gx] = packed[...]
-        return [send(packed, slots.at[gx], (i, 0, 0)) for i in range(1, sizes[0])]
+        return [send(packed, slots.at[gx], (i, 0, 0)) for i in far_first(sizes[0])]
 
     def unpack_level1(slots, target, f):
         low = tiled((lane < 64).astype(jnp.int32), 16, 128) > 0
@@ -275,11 +333,18 @@
         for k in range(8):
             work[32 * k : 32 * k + 32, :] = coefficient(f, 2 * k) + coefficient(f, 2 * k + 1)
         pack_level1(pkc, f)
+    pl.semaphore_wait(barrier, len(peers))
+    halo0 = send_halo0(
+        bdw0,
+        bdw0,
+        lambda b, planes: tt.at[0 if b == -1 else 1, planes],
+        lambda rows: ee.at[pl.ds(0, 2), rows],
+        lambda rows: ee.at[2, rows],
+        sy,
+        (sxm0, sxm1, sxm2),
+        (sxc0, sxc1, sxc2),
+    )
     coef1 = gather_gx(pkc, g1c)
-
-    finish(halo0)
-    for f in (0, 1):
-        fill_halo0(bdw0, f, sy, sxm, sxc)
 
     def send_halo1(own, target, width):
         copies = []
@@ -320,14 +385,58 @@
         unpack_level1(g1c, put, f)
     view1 = lambda a, b: c1.at[:, a, b]
     coef1 = send_halo1(view1, view1, 5)
+    half_i, half_l = iota((256, 128), 0), iota((256, 128), 1)
+    to_half = jnp.where((half_i >> 1) == half_l, 0.125, 0.0).astype(F32)
+
+    def coarsen_level1(pair):
+        for k in range(4):
+            total = pair(k)
+            for h in (0, 1):
+                work2[h, 16 * k : 16 * k + 16, :] = total[:, 128 * h : 128 * h + 128]
+        halves = [work2[h, pl.ds(0, 32, stride=2), :] + work2[h, pl.ds(1, 32, stride=2), :] for h in (0, 1)]
+        return dot(jnp.concatenate(halves, axis=1), to_half)
+
+    for f in (0, 1):
+        coarse = coarsen_level1(lambda k: c1[f, 8 + 2 * k, 0:16] + c1[f, 9 + 2 * k, 0:16])
+        for k in range(4):
+            c2[f, 8 + k, 0:8] = coarse[8 * k : 8 * k + 8]
+    view2 = lambda a, b: c2.at[:, a, b]
+    coef2 = send_halo2(view2, view2, (0, 1, -1, 2, -2))
+
+    third_lane = lane_i - jnp.where(gz >= sizes[2] // 2, 64, 0)
+    to_third = jnp.where(((row_i >> 1) == third_lane) & (third_lane >= 0) & (third_lane < 64), 0.125, 0.0)
+    to_third = to_third.astype(F32)
+
+    def coarsen_level2(pair):
+        for k in range(2):
+            work[8 * k : 8 * k + 8, :] = pair(k)
+        return dot(rows_summed(16), to_third)
+
+    def gather_gz(piece, slots):
+        slots[gz] = piece[...]
+        return [send(piece, slots.at[gz], (0, 0, i)) for i in far_first(sizes[2])]
+
+    def gather_gy(slots, packed, target, fields):
+        for f in range(fields):
+            for k in range(8):
+                packed[f, k] = slots[k, f] + slots[k + 8, f]
+        target[gy] = packed[...]
+        return [send(packed, target.at[gy], (0, i, 0)) for i in far_first(sizes[1])]
+
+    for f in (0, 1):
+        p3c[f] = coarsen_level2(lambda k: c2[f, 8 + 2 * k, 0:8] + c2[f, 9 + 2 * k, 0:8])
+    coef3 = gather_gz(p3c, z3c)
+
+    finish(halo0)
+    fill_coefficients0()
 
     bd0_at = lambda p: bdw0[0, p]
     wd0_at = lambda p: bdw0[1, p]
     no_edges = (None,) * 4
-    first_half(v0.at[0], bd0_at, 0, 24)
-    half_sweep(v0.at[0], bd0_at, wd0_at, 1, 23, 1, no_edges)
-    half_sweep(v0.at[0], bd0_at, wd0_at, 2, 22, 0, no_edges)
-    half_sweep(v0.at[0], bd0_at, wd0_at, 3, 21, 1, no_edges)
+    first_half(v0.at[0], bd0_at, 0, 24, B0)
+    half_sweep(v0.at[0], bd0_at, wd0_at, 1, 23, 1, no_edges, B0)
+    half_sweep(v0.at[0], bd0_at, wd0_at, 2, 22, 0, no_edges, B0)
+    half_sweep(v0.at[0], bd0_at, wd0_at, 3, 21, 1, no_edges, B0)
 
     def residual0(k, carry):
         total = None
@@ -343,17 +452,11 @@
     pack_level1(pk, 0)
     right1 = gather_gx(pk, g1)
 
-    ev[...] = jnp.zeros(ev.shape, F32)
-
-    def pack_v(z, carry):
+    for z in range(NZ):
         value = v0[0, z + 4, 0:NY, 0:NX]
-        pack_edges(value, tv, ev, 0, z)
+        tv[z] = jnp.where(low4, value[0:8], value[NY - 8 : NY])
         vp0[0, z + 4, 0:NY, 0:NX] = value
-        return carry
-
-    lax.fori_loop(0, NZ, pack_v, 0)
-    pack_corner(ev, 0)
-    halo_v0 = send_halo0(v0, vp0, tv, ev, syv, sxmv, sxcv)
+    ev[...] = gathered_edges(lambda z: v0[0, z + 4, 0:NY, 0:NX])
 
     finish(coef1)
 
@@ -394,24 +497,6 @@
 
     coefficients(lambda f, p: c1[f, p], wd1, in1, (3, 21), 0.25, valid1)
 
-    half_i, half_l = iota((256, 128), 0), iota((256, 128), 1)
-    to_half = jnp.where((half_i >> 1) == half_l, 0.125, 0.0).astype(F32)
-
-    def coarsen_level1(pair):
-        for k in range(4):
-            total = pair(k)
-            for h in (0, 1):
-                work2[h, 16 * k : 16 * k + 16, :] = total[:, 128 * h : 128 * h + 128]
-        halves = [work2[h, pl.ds(0, 32, stride=2), :] + work2[h, pl.ds(1, 32, stride=2), :] for h in (0, 1)]
-        return dot(jnp.concatenate(halves, axis=1), to_half)
-
-    for f in (0, 1):
-        coarse = coarsen_level1(lambda k: c1[f, 8 + 2 * k, 0:16] + c1[f, 9 + 2 * k, 0:16])
-        for k in range(4):
-            c2[f, 8 + k, 0:8] = coarse[8 * k : 8 * k + 8]
-    view2 = lambda a, b: c2.at[:, a, b]
-    coef2 = send_halo2(view2, view2, (0, 1, -1, 2, -2))
-
     finish(right1)
 
     def put_right(p, lanes, value):
@@ -420,36 +505,19 @@
     unpack_level1(g1, put_right, 0)
     view_r1 = lambda a, b: r1.at[a, b]
     right1 = send_halo1(view_r1, view_r1, 5)
+    halo_v0 = send_halo0(
+        v0,
+        vp0,
+        lambda b, planes: tv.at[planes],
+        lambda rows: ev.at[rows],
+        lambda rows: ev.at[rows],
+        syv,
+        sxmv,
+        sxcv,
+    )
 
     finish(coef2)
     coefficients(lambda f, p: c2[f, p], wd2, in2, (2, 18), 0.0625, valid2)
-
-    third_lane = lane_i - jnp.where(gz >= sizes[2] // 2, 64, 0)
-    to_third = jnp.where(((row_i >> 1) == third_lane) & (third_lane >= 0) & (third_lane < 64), 0.125, 0.0)
-    to_third = to_third.astype(F32)
-
-    def coarsen_level2(pair):
-        for k in range(2):
-            work[8 * k : 8 * k + 8, :] = pair(k)
-        return dot(rows_summed(16), to_third)
-
-    def gather_gz(piece, slots):
-        slots[gz] = piece[...]
-        return [send(piece, slots.at[gz], (0, 0, i)) for i in range(1, sizes[2])]
-
-    def gather_gy(slots, packed, target, fields):
-        for f in range(fields):
-            for k in range(8):
-                packed[f, k] = slots[k, f] + slots[k + 8, f]
-        target[gy] = packed[...]
-        return [send(packed, target.at[gy], (0, i, 0)) for i in range(1, sizes[1])]
-
-    for f in (0, 1):
-        p3c[f] = coarsen_level2(lambda k: c2[f, 8 + 2 * k, 0:8] + c2[f, 9 + 2 * k, 0:8])
-    coef3 = gather_gz(p3c, z3c)
-
-    finish(halo_v0)
-    fill_halo0(vp0, 0, syv, sxmv, sxcv)
 
     finish(right1)
 
@@ -466,10 +534,10 @@
     edges1 = (None, None, lanes1 == 0, lanes1 == 255)
     bd1_at = lambda p: bd1[p]
     wd1_at = lambda p: wd1[p]
-    first_half(v1, bd1_at, 4, 20)
-    half_sweep(v1, bd1_at, wd1_at, 5, 19, 1, edges1)
-    half_sweep(v1, bd1_at, wd1_at, 6, 18, 0, edges1)
-    half_sweep(v1, bd1_at, wd1_at, 7, 17, 1, edges1)
+    first_half(v1, bd1_at, 4, 20, B1)
+    half_sweep(v1, bd1_at, wd1_at, 5, 19, 1, edges1, B1)
+    half_sweep(v1, bd1_at, wd1_at, 6, 18, 0, edges1, B1)
+    half_sweep(v1, bd1_at, wd1_at, 7, 17, 1, edges1, B1)
 
     def residual1(k):
         total = None
@@ -491,6 +559,8 @@
     halo_v1 = send_halo1(lambda a, b: v1.at[a, b], lambda a, b: vp1.at[a, b], 6)
     finish(coef3)
     coef3 = gather_gy(z3c, y3cs, y3c, 2)
+    finish(halo_v0)
+    fill_v0()
 
     finish(right2)
     scaled(bd2, r2, in2, 4, 16)
@@ -498,10 +568,10 @@
     edges2 = (None, None, lanes2 == 0, lanes2 == 127)
     bd2_at = lambda p: bd2[p]
     wd2_at = lambda p: wd2[p]
-    first_half(v2, bd2_at, 4, 16)
-    half_sweep(v2, bd2_at, wd2_at, 5, 15, 1, edges2)
-    half_sweep(v2, bd2_at, wd2_at, 6, 14, 0, edges2)
-    half_sweep(v2, bd2_at, wd2_at, 7, 13, 1, edges2)
+    first_half(v2, bd2_at, 4, 16, B2)
+    half_sweep(v2, bd2_at, wd2_at, 5, 15, 1, edges2, B2)
+    half_sweep(v2, bd2_at, wd2_at, 6, 14, 0, edges2, B2)
+    half_sweep(v2, bd2_at, wd2_at, 7, 13, 1, edges2, B2)
 
     def residual2(k):
         total = None
@@ -591,13 +661,13 @@
 
     def half3(colour):
         ends(v3, 16)
-        half_sweep(v3, bd3_at, wd3_at, 1, 17, colour, edges3, 1)
+        half_sweep(v3, bd3_at, wd3_at, 1, 17, colour, edges3, 16, 1)
 
     def half4(colour):
         ends(v4, 8)
-        half_sweep(v4, bd4_at, wd4_at, 1, 9, colour, edges4, 1)
-
-    first_half(v3, bd3_at, 1, 17, 1)
+        half_sweep(v4, bd4_at, wd4_at, 1, 9, colour, edges4, 8, 1)
+
+    first_half(v3, bd3_at, 1, 17, 16, 1)
     half3(1)
     half3(0)
     half3(1)
@@ -615,7 +685,7 @@
     coarse = coarsen_level3(residual3)
     for k in range(8):
         bd4[k] = coarse[16 * k : 16 * k + 16] * in4[k]
-    first_half(v4, bd4_at, 1, 9, 1)
+    first_half(v4, bd4_at, 1, 9, 8, 1)
     half4(1)
 
     def sweep4(i, carry):
@@ -671,10 +741,10 @@
         return carry
 
     lax.fori_loop(0, 10, add2, 0)
-    half_sweep(vp2, bd2_at, wd2_at, 2, 18, 0, edges2)
-    half_sweep(vp2, bd2_at, wd2_at, 3, 17, 1, edges2)
-    half_sweep(vp2, bd2_at, wd2_at, 4, 16, 0, edges2)
-    half_sweep(vp2, bd2_at, wd2_at, 5, 15, 1, edges2)
+    half_sweep(vp2, bd2_at, wd2_at, 2, 18, 0, edges2, B2)
+    half_sweep(vp2, bd2_at, wd2_at, 3, 17, 1, edges2, B2)
+    half_sweep(vp2, bd2_at, wd2_at, 4, 16, 0, edges2, B2)
+    half_sweep(vp2, bd2_at, wd2_at, 5, 15, 1, edges2, B2)
 
     def spread(wide, rows):
         for h in (0, 1):
@@ -700,10 +770,10 @@
         return carry
 
     lax.fori_loop(0, 10, add1, 0)
-    half_sweep(vp1, bd1_at, wd1_at, 3, 21, 0, edges1)
-    half_sweep(vp1, bd1_at, wd1_at, 4, 20, 1, edges1)
-    half_sweep(vp1, bd1_at, wd1_at, 5, 19, 0, edges1)
-    half_sweep(vp1, bd1_at, wd1_at, 6, 18, 1, edges1)
+    half_sweep(vp1, bd1_at, wd1_at, 3, 21, 0, edges1, B1)
+    half_sweep(vp1, bd1_at, wd1_at, 4, 20, 1, edges1, B1)
+    half_sweep(vp1, bd1_at, wd1_at, 5, 19, 0, edges1, B1)
+    half_sweep(vp1, bd1_at, wd1_at, 6, 18, 1, edges1, B1)
 
     first_i, first_l = iota((256, 256), 0), iota((256, 256), 1)
     column = jnp.where(first_l < NX + 4, first_l, jnp.where(first_l >= 2 * NX - 4, first_l - 2 * NX, -1024))
@@ -722,36 +792,48 @@
         return carry
 
     lax.fori_loop(0, 12, add0, 0)
-    half_sweep(vp0.at[0], bd0_at, wd0_at, 1, 23, 0, no_edges)
-    half_sweep(vp0.at[0], bd0_at, wd0_at, 2, 22, 1, no_edges)
-    half_sweep(vp0.at[0], bd0_at, wd0_at, 3, 21, 0, no_edges)
+    half_sweep(vp0.at[0], bd0_at, wd0_at, 1, 23, 0, no_edges, B0)
+    half_sweep(vp0.at[0], bd0_at, wd0_at, 2, 22, 1, no_edges, B0)
+    half_sweep(vp0.at[0], bd0_at, wd0_at, 3, 21, 0, no_edges, B0)
     par = parity_of(NY, NX)
 
-    def last(p, odd):
-        c, s = neighbours(vp0.at[0], p, no_edges)
-        new = bdw0[0, p, 0:NY, 0:NX] + bdw0[1, p, 0:NY, 0:NX] * s[0:NY, 0:NX]
-        out[p - 4] = jnp.where(par == ((odd + 1) & 1), new, c[0:NY, 0:NX])
-
-    pairs(4, 20, last)
+    def last(first, odd, size):
+        before, c = vp0[0, first - 1], vp0[0, first]
+        for i in range(size):
+            p = first + i
+            behind = vp0[0, p + 1]
+            s = neighbour_sum(before, c, behind, no_edges)
+            new = bdw0[0, p, 0:NY, 0:NX] + bdw0[1, p, 0:NY, 0:NX] * s[0:NY, 0:NX]
+            out[p - 4] = jnp.where(par == ((odd + i + 1) & 1), new, c[0:NY, 0:NX])
+            before, c = c, behind
+
+    blocks(4, 20, B0, last)
 
 
 def local(sizes, source, labels):
     vmem = lambda *shape: pltpu.VMEM(shape, F32)
     scratch = [
+        vmem(16, 32, 128),
+        pltpu.VMEM((16, 32, 128), jnp.int32),
+        pltpu.SemaphoreType.DMA((2,)),
         vmem(2, 24, 40, 256),
         vmem(1, 24, 40, 256),
         vmem(1, 24, 40, 256),
         vmem(16, 32, 128),
         vmem(2, 16, 8, 128),
-        vmem(2, 40, 128),
-        vmem(1, 16, 8, 128),
-        vmem(1, 40, 128),
-        vmem(2, 2, 24, 8, 128),
-        vmem(2, 1, 24, 8, 128),
-        vmem(2, 3, 2, 32, 128),
-        vmem(2, 3, 2, 2, 8, 128),
-        vmem(2, 3, 1, 32, 128),
-        vmem(2, 3, 2, 1, 8, 128),
+        vmem(3, 40, 128),
+        vmem(16, 8, 128),
+        vmem(40, 128),
+        vmem(2, 24, 8, 128),
+        vmem(2, 24, 8, 128),
+        vmem(2, 32, 128),
+        vmem(2, 2, 32, 128),
+        vmem(2, 32, 128),
+        vmem(2, 2, 8, 128),
+        vmem(2, 2, 2, 8, 128),
+        vmem(2, 2, 8, 128),
+        *[vmem(2, 32, 128)] * 3,
+        *[vmem(2, 2, 8, 128)] * 3,
         vmem(1, 64, 128),
         vmem(2, 64, 128),
         vmem(sizes[0], 1, 64, 128),
@@ -796,7 +878,7 @@
     return pl.pallas_call(
         functools.partial(kernel, sizes),
         out_shape=jax.ShapeDtypeStruct(source.shape, F32),
-        in_specs=[pl.BlockSpec(memory_space=pltpu.VMEM)] * 2,
+        in_specs=[pl.BlockSpec(memory_space=pltpu.HBM)] * 2,
         out_specs=pl.BlockSpec(memory_space=pltpu.VMEM),
         scratch_shapes=scratch,
         compiler_params=pltpu.CompilerParams(

time: 108 us -> 83.6 us (0.77)
  Pallas kernels: 105 us -> 80.9 us
    pallas_call x1, Pallas kernels: 105 us -> 80.9 us  [local(): pl.pallas_call(functools.partial(kernel, sizes), out_shape=jax.ShapeDtype...]
where the time goes in v2:
time: 83.6 us; the launch traced here: 83.5 us
  Pallas kernels  80.9 us (97%)
  local copies, waits for them, and re-layouts  2.6 us (3%)
    pallas_call x1, Pallas kernels, local(): pl.pallas_call(functools.partial(kernel, sizes), out_shape=jax.ShapeDtype...  80.9 us
    unnamed x5, local copies, waits for them, and re-layouts  2.6 us

profile of v2, /device:TPU:1, one launch (start us, length us, event | category | flops | bytes accessed | tf_op | source)
XLA Modules:
  0.0 83.5 jit_solution(8888204341578645204)
XLA Ops:
  0.0 0.0 copy-start
  0.0 0.9 %copy-done = f32[16,32,128]{2,1,0:T(8,128)S(1)} copy-done((f32[16,32,128]{2,1,0:T(8,128)S(1)}, f32[16,32,128]{2,1,0:T(8,128)}, u32[]{:S(2)}) %copy-start) | copy-done | bytes 262168
  1.0 0.0 copy-start.1
  1.0 0.9 %copy-done.1 = s32[16,32,128]{2,1,0:T(8,128)S(1)} copy-done((s32[16,32,128]{2,1,0:T(8,128)S(1)}, s32[16,32,128]{2,1,0:T(8,128)}, u32[]{:S(2)}) %copy-start.1) | copy-done | bytes 262168
  1.9 80.9 %v_cycle.1 = f32[16,32,128]{2,1,0:T(8,128)S(1)} custom-call(f32[16,32,128]{2,1,0:T(8,128)S(1)} %copy-done, s32[16,32,128]{2,1,0:T(8,128)S(1)} %copy-done.1), custom_call_target="tpu_custom_call" | custom-call | tf_op jit(solution)/shard_map/v_cycle/pallas_call | solution.py:878
  82.8 0.7 copy.4
Async XLA Ops:
  0.0 0.9 %copy-start = (f32[16,32,128]{2,1,0:T(8,128)S(1)}, f32[16,32,128]{2,1,0:T(8,128)}, u32[]{:S(2)}) copy-start(f32[16,32,128]{2,1,0:T(8,128)} %refs_0_.1) | copy-start | bytes 786436
  1.0 0.9 %copy-start.1 = (s32[16,32,128]{2,1,0:T(8,128)S(1)}, s32[16,32,128]{2,1,0:T(8,128)}, u32[]{:S(2)}) copy-start(s32[16,32,128]{2,1,0:T(8,128)} %refs_1_.1) | copy-start | bytes 786436

commit v3 on v2

--- a/solution.py
+++ b/solution.py
@@ -15,7 +15,7 @@
 MESH = pl.DeviceIdType.MESH
 HIGHEST = lax.Precision.HIGHEST
 F32 = jnp.float32
-COPIES = 176
+COPIES = 128
 
 B0, B1, B2 = 8, 10, 16
 
@@ -107,11 +107,10 @@
 
 
 def kernel(sizes, *refs):
-    (source_hbm, labels_hbm, out, source, labels, isem, bdw0, v0, vp0, d0, tt, ee, tv, ev, sy, syv, sxm0, sxm1, sxm2, sxc0, sxc1, sxc2, *rest) = refs
-    (sxmv0, sxmv1, sxmv2, sxcv0, sxcv1, sxcv2, pk, pkc, g1, g1c,
+    (source_hbm, labels_hbm, out, source, labels, isem, bdw0, v0, vp0, d0, tt, ee, tv, ev, sy, syv, sxm0, sxm1, sxm2, sxc0, sxc1, sxc2, sxv, *rest) = refs
+    ( pk, pkc, g1, g1c,
      c1, r1, v1, vp1, bd1, wd1, in1, c2, r2, v2, vp2, bd2, wd2, in2, z3, z3c, y3s, y3cs, y3, y3c, p3, p3c,
-     c3, v3, bd3, wd3, in3, c4, v4, bd4, wd4, in4, work, work2, ssem, rsem) = rest
-    sxmv, sxcv = (sxmv0, sxmv1, sxmv2), (sxcv0, sxcv1, sxcv2)
+     c3, v3, bd3, wd3, in3, c4, v4, bd4, wd4, in4, work, work2, token, ssem, rsem) = rest
     count = dict(gx=sizes[0], gy=sizes[1], gz=sizes[2])
     gx, gy, gz = lax.axis_index("gx"), lax.axis_index("gy"), lax.axis_index("gz")
     number = [0]
@@ -123,6 +122,9 @@
         )
 
     def send(source_ref, target_ref, offset):
+        return send_to(source_ref, target_ref, device(offset))
+
+    def send_to(source_ref, target_ref, target):
         i = number[0]
         number[0] += 1
         copy = pltpu.make_async_remote_copy(
@@ -130,7 +132,7 @@
             dst_ref=target_ref,
             send_sem=ssem.at[i],
             recv_sem=rsem.at[i],
-            device_id=device(offset),
+            device_id=target,
             device_id_type=MESH,
         )
         copy.start()
@@ -152,12 +154,17 @@
         peers.add((i, 0, 0))
     for i in range(1, sizes[1]):
         peers.add((0, i, 0))
-    for i in range(1, sizes[2]):
-        peers.add((0, 0, i))
     peers = sorted({tuple(step % size for step, size in zip(o, sizes)) for o in peers} - {(0, 0, 0)})
     barrier = pltpu.get_barrier_semaphore()
     for offset in peers:
         pl.semaphore_signal(barrier, inc=1, device_id=device(offset), device_id_type=MESH)
+
+    def tokens(level):
+        for step in (2 << level, -(2 << level)):
+            pl.semaphore_signal(token.at[level], inc=1, device_id=device((0, 0, step)), device_id_type=MESH)
+
+    def wait_tokens(level):
+        pl.semaphore_wait(token.at[level], 2)
 
     loads = [
         pltpu.make_async_copy(labels_hbm, labels, isem.at[0]),
@@ -181,13 +188,15 @@
         choose = lambda t: jnp.where(label == 1, t[1], jnp.where(label == 0, t[0], t[2])).astype(F32)
         return choose(inverse), choose(permittivity * inverse), choose(diagonal)
 
-    group = tiled(lane >> 3, NY, 128)
-
-    def gathered_edges(plane):
-        total = jnp.zeros((NY, 128), F32)
-        for z in range(NZ):
-            total = jnp.where(group == z, pltpu.roll(plane(z), 8 * z + 4, 1), total)
-        return jnp.concatenate([total, jnp.where(low4, total[0:8], total[NY - 8 : NY])], axis=0)
+    def gathered_edges(plane, rows=NY, planes=NZ):
+        group = tiled(lane >> 3, rows, 128)
+        total = jnp.zeros((rows, 128), F32)
+        for z in range(planes):
+            total = jnp.where(group == z, pltpu.roll(plane(z), (8 * z + 4) % 128, 1), total)
+        return total
+
+    def with_corners(edges):
+        return jnp.concatenate([edges, jnp.where(low4, edges[0:8], edges[NY - 8 : NY])], axis=0)
 
     for load in loads:
         load.wait()
@@ -199,8 +208,8 @@
         bdw0[1, z + 4, 0:NY, 0:NX] = relative
         tt[0, z] = jnp.where(low4, bd[0:8], pltpu.roll(relative[0:8], 4, 0))
         tt[1, z] = jnp.where(low4, pltpu.roll(relative[NY - 8 : NY], 4, 0), bd[NY - 8 : NY])
-    edge_bd = gathered_edges(lambda z: bdw0[0, z + 4, 0:NY, 0:NX])
-    edge_wd = gathered_edges(lambda z: bdw0[1, z + 4, 0:NY, 0:NX])
+    edge_bd = with_corners(gathered_edges(lambda z: bdw0[0, z + 4, 0:NY, 0:NX]))
+    edge_wd = with_corners(gathered_edges(lambda z: bdw0[1, z + 4, 0:NY, 0:NX]))
     ee[0], ee[1] = edge_bd, edge_wd
     quarter = tiled(lane >> 5, NY + 8, 128)
     inner = jnp.where(quarter == 1, pltpu.roll(edge_wd, 32, 1), pltpu.roll(edge_wd, 96, 1))
@@ -289,13 +298,23 @@
 
             fill_halo0(bdw0, f, rows_of, columns, ((12, 0, 0), (8, 0, 4))[f])
 
+    x_side = jnp.where(in_low_half, x_hi.astype(jnp.int32), x_lo.astype(jnp.int32))
+    y_side = jnp.where(low4, y_hi.astype(jnp.int32), y_lo.astype(jnp.int32))
+
     def fill_v0():
-        def columns(part):
-            m, c = sxmv[part], sxcv[part]
-            return [(m[s], c[s, 1], c[s, 0]) for s in (1, 0)]
-
-        fill_halo0(vp0, 0, lambda p: jnp.where(low4, syv[1, p], syv[0, p]), columns, (12, 0, 0))
-
+        right = tiled(in_low_half.astype(jnp.int32), NY + 8, 128) > 0
+        valid = tiled(x_side, NY + 8, 128) > 0
+        edges = tiled(((lane < 4) | (lane >= 124)).astype(jnp.int32), NY + 8, 128) > 0
+        packed = [jnp.where(valid, jnp.where(right, sxv[1, j], sxv[0, j]), 0.0) for j in (0, 1)]
+        for p in range(NZ + 8):
+            rolled = pltpu.roll(packed[p // 16], 124 - 8 * (p % 16), 1)
+            vp0[0, p, :, NX : 2 * NX] = jnp.where(edges, rolled, 0.0)
+        for first, inside in ((0, z_lo), (NZ + 4, z_hi)):
+
+            @pl.when(jnp.logical_not(inside))
+            def _():
+                for p in range(first, first + 4):
+                    vp0[0, p] = jnp.zeros((NY + 8, 2 * NX), F32)
 
     row_i, lane_i = iota((128, 128), 0), iota((128, 128), 1)
     to_low = jnp.where((row_i >> 1) == lane_i, 0.125, 0.0).astype(F32)
@@ -345,6 +364,7 @@
         (sxc0, sxc1, sxc2),
     )
     coef1 = gather_gx(pkc, g1c)
+    tokens(0)
 
     def send_halo1(own, target, width):
         copies = []
@@ -362,6 +382,35 @@
                     )
         return copies
 
+    def send_z1(own, target, width):
+        return [
+            send(
+                own(pl.ds(16 - width if c == 1 else 8, width), pl.ds(0, 16)),
+                target(pl.ds(8 - width if c == 1 else 16, width), pl.ds(0, 16)),
+                (0, 0, c),
+            )
+            for c in (1, -1)
+        ]
+
+    def send_y1(view, width):
+        planes = pl.ds(8 - width, 8 + 2 * width)
+        return [
+            send(view(planes, pl.ds(8 if b == 1 else 0, 8)), view(planes, pl.ds(24 if b == 1 else 16, 8)), (0, b, 0))
+            for b in (1, -1)
+        ]
+
+    def send_z2(own, target):
+        return [
+            send(own(pl.ds(8, 4), pl.ds(0, 8)), target(pl.ds(8 - 4 * c, 4), pl.ds(0, 8)), (0, 0, c))
+            for c in (2, -2, 1, -1)
+        ]
+
+    def send_y2(view):
+        planes = pl.ds(0, 20)
+        return [
+            send(view(planes, pl.ds(0, 8)), view(planes, pl.ds(16 if b == 1 else 8, 8)), (0, b, 0)) for b in (1, -1)
+        ]
+
     def send_halo2(own, target, steps):
         copies = []
         for c in steps:
@@ -384,7 +433,7 @@
 
         unpack_level1(g1c, put, f)
     view1 = lambda a, b: c1.at[:, a, b]
-    coef1 = send_halo1(view1, view1, 5)
+    coef1 = send_z1(view1, view1, 5)
     half_i, half_l = iota((256, 128), 0), iota((256, 128), 1)
     to_half = jnp.where((half_i >> 1) == half_l, 0.125, 0.0).astype(F32)
 
@@ -400,34 +449,34 @@
         coarse = coarsen_level1(lambda k: c1[f, 8 + 2 * k, 0:16] + c1[f, 9 + 2 * k, 0:16])
         for k in range(4):
             c2[f, 8 + k, 0:8] = coarse[8 * k : 8 * k + 8]
-    view2 = lambda a, b: c2.at[:, a, b]
-    coef2 = send_halo2(view2, view2, (0, 1, -1, 2, -2))
-
-    third_lane = lane_i - jnp.where(gz >= sizes[2] // 2, 64, 0)
-    to_third = jnp.where(((row_i >> 1) == third_lane) & (third_lane >= 0) & (third_lane < 64), 0.125, 0.0)
-    to_third = to_third.astype(F32)
-
-    def coarsen_level2(pair):
+
+    half_gz = jnp.where(gz >= sizes[2] // 2, 64, 0)
+
+    def to_third(offset):
+        return jnp.where((row_i >> 1) == lane_i - offset, 0.125, 0.0).astype(F32)
+
+    def coarsen_level2(pair, matrix):
         for k in range(2):
             work[8 * k : 8 * k + 8, :] = pair(k)
-        return dot(rows_summed(16), to_third)
+        return dot(rows_summed(16), matrix)
 
     def gather_gz(piece, slots):
         slots[gz] = piece[...]
         return [send(piece, slots.at[gz], (0, 0, i)) for i in far_first(sizes[2])]
 
-    def gather_gy(slots, packed, target, fields):
-        for f in range(fields):
-            for k in range(8):
-                packed[f, k] = slots[k, f] + slots[k + 8, f]
+    def gather_gy(packed, target):
         target[gy] = packed[...]
         return [send(packed, target.at[gy], (0, i, 0)) for i in far_first(sizes[1])]
 
-    for f in (0, 1):
-        p3c[f] = coarsen_level2(lambda k: c2[f, 8 + 2 * k, 0:8] + c2[f, 9 + 2 * k, 0:8])
-    coef3 = gather_gz(p3c, z3c)
+    view2 = lambda a, b: c2.at[:, a, b]
+    coef2 = send_z2(view2, view2)
+    p3c[...] = coarsen_level2(lambda k: c2[0, 8 + 2 * k, 0:8] + c2[0, 9 + 2 * k, 0:8], to_third(0)) + coarsen_level2(
+        lambda k: c2[1, 8 + 2 * k, 0:8] + c2[1, 9 + 2 * k, 0:8], to_third(64)
+    )
 
     finish(halo0)
+    wait_tokens(0)
+    tokens(1)
     fill_coefficients0()
 
     bd0_at = lambda p: bdw0[0, p]
@@ -445,20 +494,28 @@
             value = bdw0[0, p, 0:NY, 0:NX] - c[0:NY, 0:NX] + bdw0[1, p, 0:NY, 0:NX] * s[0:NY, 0:NX]
             value = d0[p - 4] * value
             total = value if total is None else total + value
-        work[pl.ds(pl.multiple_of(32 * k, 32), 32), :] = total
+        work[pl.ds(32 * k, 32), :] = total
         return carry
 
-    lax.fori_loop(0, 8, residual0, 0)
+    for k in range(8):
+        residual0(k, 0)
     pack_level1(pk, 0)
     right1 = gather_gx(pk, g1)
 
+    view_v0 = lambda ref, first: ref.at[0, pl.ds(first, 4), pl.ds(0, NY), pl.ds(0, NX)]
+    halo_v0 = [
+        send(view_v0(v0, 16), view_v0(vp0, 0), (0, 0, 1)),
+        send(view_v0(v0, 4), view_v0(vp0, 20), (0, 0, -1)),
+    ]
+    finish(coef1)
+    coef1 = send_y1(view1, 5)
+    finish(coef2)
+    coef2 = send_y2(view2)
+    wait_tokens(1)
+    coef3 = gather_gz(p3c, z3c)
     for z in range(NZ):
-        value = v0[0, z + 4, 0:NY, 0:NX]
-        tv[z] = jnp.where(low4, value[0:8], value[NY - 8 : NY])
-        vp0[0, z + 4, 0:NY, 0:NX] = value
-    ev[...] = gathered_edges(lambda z: v0[0, z + 4, 0:NY, 0:NX])
-
-    finish(coef1)
+        vp0[0, z + 4, 0:NY, 0:NX] = v0[0, z + 4, 0:NY, 0:NX]
+
 
     def row_valid(rows, own):
         tiles = [jnp.ones((8, 128), jnp.int32)] * (own // 8)
@@ -482,7 +539,8 @@
             wd_at[p] = weight * inverse
             return carry
 
-        lax.fori_loop(planes[0], planes[1], body, 0)
+        for p in range(*planes):
+            body(p, 0)
 
     rows1 = jnp.concatenate([row_valid(32, 16)] * 2, axis=1)
     rows2 = row_valid(24, 8)
@@ -495,8 +553,6 @@
         ok = jnp.where(z >= 0, 1, 0) * jnp.where(z < 4 * sizes[2], 1, 0)
         return rows2 * ok
 
-    coefficients(lambda f, p: c1[f, p], wd1, in1, (3, 21), 0.25, valid1)
-
     finish(right1)
 
     def put_right(p, lanes, value):
@@ -505,17 +561,13 @@
     unpack_level1(g1, put_right, 0)
     view_r1 = lambda a, b: r1.at[a, b]
     right1 = send_halo1(view_r1, view_r1, 5)
-    halo_v0 = send_halo0(
-        v0,
-        vp0,
-        lambda b, planes: tv.at[planes],
-        lambda rows: ev.at[rows],
-        lambda rows: ev.at[rows],
-        syv,
-        sxmv,
-        sxcv,
-    )
-
+
+    finish(halo_v0)
+    for z in range(NZ + 8):
+        tv[z] = jnp.where(low4, vp0[0, z, 0:8, 0:NX], vp0[0, z, NY - 8 : NY, 0:NX])
+    halo_v0 = [send(tv, syv.at[0 if b == 1 else 1], (0, b, 0)) for b in (1, -1)]
+    finish(coef1)
+    coefficients(lambda f, p: c1[f, p], wd1, in1, (3, 21), 0.25, valid1)
     finish(coef2)
     coefficients(lambda f, p: c2[f, p], wd2, in2, (2, 18), 0.0625, valid2)
 
@@ -526,7 +578,8 @@
             target[p] = right[p] * inverse[p]
             return carry
 
-        lax.fori_loop(start, stop, body, 0)
+        for p in range(start, stop):
+            body(p, 0)
 
     scaled(bd1, r1, in1, 3, 21)
     lanes1 = jnp.concatenate([lane, lane + 128], axis=1)
@@ -548,6 +601,7 @@
             total = value if total is None else total + value
         return total
 
+    to_third_own = jnp.where((lane_i - half_gz >= 0) & (lane_i - half_gz < 64), to_third(half_gz), 0.0)
     coarse = coarsen_level1(residual1)
     for k in range(4):
         r2[8 + k, 0:8] = coarse[8 * k : 8 * k + 8]
@@ -556,11 +610,21 @@
     right2_far = send_halo2(view_r2, view_r2, (2, -2))
     for k in range(8):
         vp1[8 + k, 0:16] = v1[8 + k, 0:16]
-    halo_v1 = send_halo1(lambda a, b: v1.at[a, b], lambda a, b: vp1.at[a, b], 6)
+    halo_v1 = send_z1(lambda a, b: v1.at[a, b], lambda a, b: vp1.at[a, b], 6)
     finish(coef3)
-    coef3 = gather_gy(z3c, y3cs, y3c, 2)
+    low8 = lane < 64
+    for k in range(8):
+        a, b = z3c[k], z3c[k + 8]
+        y3cs[0, k] = jnp.where(low8, a, pltpu.roll(b, 64, 1))
+        y3cs[1, k] = jnp.where(low8, pltpu.roll(a, 64, 1), b)
+    coef3 = gather_gy(y3cs, y3c)
     finish(halo_v0)
-    fill_v0()
+    for p in range(NZ + 8):
+        rows = jnp.where(low4, syv[1, p], syv[0, p])
+        vp0[0, p, NY : NY + 8, 0:NX] = jnp.where(y_side > 0, rows, 0.0)
+    ev[0] = gathered_edges(lambda z: vp0[0, z, :, 0:NX], NY + 8, 16)
+    ev[1] = gathered_edges(lambda z: vp0[0, z + 16, :, 0:NX], NY + 8, 8)
+    halo_v0 = [send(ev, sxv.at[0 if a == 1 else 1], (a, 0, 0)) for a in (1, -1)]
 
     finish(right2)
     scaled(bd2, r2, in2, 4, 16)
@@ -582,11 +646,13 @@
             total = value if total is None else total + value
         return total
 
-    p3[0] = coarsen_level2(residual2)
+    p3[...] = coarsen_level2(residual2, to_third_own)
     right3 = gather_gz(p3, z3)
     for k in range(4):
         vp2[8 + k, 0:8] = v2[8 + k, 0:8]
-    halo_v2 = send_halo2(lambda a, b: v2.at[a, b], lambda a, b: vp2.at[a, b], (0, 1, -1, 2, -2))
+    halo_v2 = send_z2(lambda a, b: v2.at[a, b], lambda a, b: vp2.at[a, b])
+    finish(halo_v1)
+    halo_v1 = send_y1(lambda a, b: vp1.at[a, b], 6)
 
     finish(coef3)
 
@@ -622,19 +688,26 @@
     finish(right2_far)
     scaled(bd2, r2, in2, 2, 4)
     scaled(bd2, r2, in2, 16, 18)
-    finish(halo_v1)
 
     def clean(target, valid, start, stop):
         def body(p, carry):
             target[p] = jnp.where(valid(p) > 0, target[p], 0.0)
             return carry
 
-        lax.fori_loop(start, stop, body, 0)
-
+        for p in range(start, stop):
+            body(p, 0)
+
+    finish(halo_v0)
+    fill_v0()
+    finish(halo_v2)
+    halo_v2 = send_y2(lambda a, b: vp2.at[a, b])
+    finish(halo_v1)
     clean(vp1, valid1, 2, 22)
 
     finish(right3)
-    right3 = gather_gy(z3, y3s, y3, 1)
+    for k in range(8):
+        y3s[0, k] = z3[k] + z3[k + 8]
+    right3 = gather_gy(y3s, y3)
     finish(halo_v2)
     clean(vp2, valid2, 0, 20)
     finish(right3)
@@ -704,12 +777,13 @@
     work[pl.ds(1, 128, stride=2), :] = wide
 
     def add3(k, carry):
-        correction = work[pl.ds(pl.multiple_of(32 * k, 32), 32), :]
+        correction = work[pl.ds(32 * k, 32), :]
         v3[1 + 2 * k] = v3[1 + 2 * k] + correction
         v3[2 + 2 * k] = v3[2 + 2 * k] + correction
         return carry
 
-    lax.fori_loop(0, 8, add3, 0)
+    for i in range(8):
+        add3(i, 0)
     half3(0)
     half3(1)
     half3(0)
@@ -733,14 +807,14 @@
     before_row = pl.multiple_of(8 * jnp.maximum(gy - 1, 0), 8)
 
     def add2(i, carry):
-        base = pl.multiple_of(64 * i, 64)
-        parts = [work[pl.ds(base + row, 8), :] for row in (own_row, next_row, before_row)]
+        parts = [work[pl.ds(64 * i + row, 8), :] for row in (own_row, next_row, before_row)]
         correction = jnp.where(rows2 > 0, jnp.concatenate(parts, axis=0), 0.0)
         vp2[2 * i] = vp2[2 * i] + correction
         vp2[2 * i + 1] = vp2[2 * i + 1] + correction
         return carry
 
-    lax.fori_loop(0, 10, add2, 0)
+    for i in range(10):
+        add2(i, 0)
     half_sweep(vp2, bd2_at, wd2_at, 2, 18, 0, edges2, B2)
     half_sweep(vp2, bd2_at, wd2_at, 3, 17, 1, edges2, B2)
     half_sweep(vp2, bd2_at, wd2_at, 4, 16, 0, edges2, B2)
@@ -764,12 +838,13 @@
     spread(wide, 160)
 
     def add1(i, carry):
-        correction = copied(pl.multiple_of(32 * i, 32), 32)
+        correction = copied(32 * i, 32)
         vp1[2 + 2 * i] = vp1[2 + 2 * i] + correction
         vp1[3 + 2 * i] = vp1[3 + 2 * i] + correction
         return carry
 
-    lax.fori_loop(0, 10, add1, 0)
+    for i in range(10):
+        add1(i, 0)
     half_sweep(vp1, bd1_at, wd1_at, 3, 21, 0, edges1, B1)
     half_sweep(vp1, bd1_at, wd1_at, 4, 20, 1, edges1, B1)
     half_sweep(vp1, bd1_at, wd1_at, 5, 19, 0, edges1, B1)
@@ -786,12 +861,13 @@
     spread(wide, 288)
 
     def add0(i, carry):
-        correction = copied(pl.multiple_of(48 * i, 16), 40)
+        correction = copied(48 * i, 40)
         vp0[0, 2 * i] = vp0[0, 2 * i] + correction
         vp0[0, 2 * i + 1] = vp0[0, 2 * i + 1] + correction
         return carry
 
-    lax.fori_loop(0, 12, add0, 0)
+    for i in range(12):
+        add0(i, 0)
     half_sweep(vp0.at[0], bd0_at, wd0_at, 1, 23, 0, no_edges, B0)
     half_sweep(vp0.at[0], bd0_at, wd0_at, 2, 22, 1, no_edges, B0)
     half_sweep(vp0.at[0], bd0_at, wd0_at, 3, 21, 0, no_edges, B0)
@@ -822,8 +898,8 @@
         vmem(16, 32, 128),
         vmem(2, 16, 8, 128),
         vmem(3, 40, 128),
-        vmem(16, 8, 128),
-        vmem(40, 128),
+        vmem(24, 8, 128),
+        vmem(2, 40, 128),
         vmem(2, 24, 8, 128),
         vmem(2, 24, 8, 128),
         vmem(2, 32, 128),
@@ -832,8 +908,7 @@
         vmem(2, 2, 8, 128),
         vmem(2, 2, 2, 8, 128),
         vmem(2, 2, 8, 128),
-        *[vmem(2, 32, 128)] * 3,
-        *[vmem(2, 2, 8, 128)] * 3,
+        vmem(2, 2, 40, 128),
         vmem(1, 64, 128),
         vmem(2, 64, 128),
         vmem(sizes[0], 1, 64, 128),
@@ -852,14 +927,14 @@
         vmem(20, 24, 128),
         vmem(20, 24, 128),
         vmem(20, 24, 128),
-        vmem(sizes[2], 1, 8, 128),
-        vmem(sizes[2], 2, 8, 128),
+        vmem(sizes[2], 8, 128),
+        vmem(sizes[2], 8, 128),
         vmem(1, 8, 8, 128),
         vmem(2, 8, 8, 128),
         vmem(sizes[1], 1, 8, 8, 128),
         vmem(sizes[1], 2, 8, 8, 128),
-        vmem(1, 8, 128),
-        vmem(2, 8, 128),
+        vmem(8, 128),
+        vmem(8, 128),
         vmem(2, 16, 32, 128),
         vmem(18, 32, 128),
         vmem(16, 32, 128),
@@ -872,6 +947,7 @@
         vmem(8, 16, 128),
         vmem(640, 128),
         vmem(2, 576, 128),
+        pltpu.SemaphoreType.REGULAR((2,)),
         pltpu.SemaphoreType.DMA((COPIES,)),
         pltpu.SemaphoreType.DMA((COPIES,)),
     ]
@@ -882,7 +958,7 @@
         out_specs=pl.BlockSpec(memory_space=pltpu.VMEM),
         scratch_shapes=scratch,
         compiler_params=pltpu.CompilerParams(
-            collective_id=0, has_side_effects=True, vmem_limit_bytes=48 * 2**20
+            collective_id=0, has_side_effects=True, vmem_limit_bytes=62 * 2**20
         ),
         name="v_cycle",
     )(source, labels)

time: 83.6 us -> 69.7 us (0.83)
  Pallas kernels: 80.9 us -> 67.9 us
  local copies, waits for them, and re-layouts: 2.6 us -> 1.67 us
    pallas_call x1, Pallas kernels: 80.9 us -> 67.9 us  [local(): pl.pallas_call(functools.partial(kernel, sizes), out_shape=jax.ShapeDtype...]
    unnamed x5 -> x1, local copies, waits for them, and re-layouts: 2.6 us -> 1.67 us
where the time goes in v3:
time: 69.7 us; the launch traced here: 69.6 us
  Pallas kernels  67.9 us (97%)
  local copies, waits for them, and re-layouts  1.67 us (2%)
    pallas_call x1, Pallas kernels, local(): pl.pallas_call(functools.partial(kernel, sizes), out_shape=jax.ShapeDtype...  67.9 us
    unnamed x1, local copies, waits for them, and re-layouts  1.67 us

profile of v3, /device:TPU:1, one launch (start us, length us, event | category | flops | bytes accessed | tf_op | source)
XLA Modules:
  0.0 69.6 jit_solution(10126602689078347110)
XLA Ops:
  0.0 67.9 %v_cycle.1 = f32[16,32,128]{2,1,0:T(8,128)} custom-call(f32[16,32,128]{2,1,0:T(8,128)} %refs_0_.1, s32[16,32,128]{2,1,0:T(8,128)} %refs_1_.1), custom_call_target="tpu_custom_call" | custom-call | tf_op jit(solution)/shard_map/v_cycle/pallas_call | solution.py:954
  67.9 1.7 %copy.4 = f32[16,32,128]{2,1,0:T(8,128)} copy(f32[16,32,128]{2,1,0:T(8,128)} %v_cycle.1) | data formatting | bytes 524288

commit v4 on v3

--- a/solution.py
+++ b/solution.py
@@ -17,7 +17,7 @@
 F32 = jnp.float32
 COPIES = 128
 
-B0, B1, B2 = 8, 10, 16
+B0, B1, B2 = 24, 24, 16
 
 NZ, NY, NX = 16, 32, 128
 
@@ -109,7 +109,7 @@
 def kernel(sizes, *refs):
     (source_hbm, labels_hbm, out, source, labels, isem, bdw0, v0, vp0, d0, tt, ee, tv, ev, sy, syv, sxm0, sxm1, sxm2, sxc0, sxc1, sxc2, sxv, *rest) = refs
     ( pk, pkc, g1, g1c,
-     c1, r1, v1, vp1, bd1, wd1, in1, c2, r2, v2, vp2, bd2, wd2, in2, z3, z3c, y3s, y3cs, y3, y3c, p3, p3c,
+     c1, r1, v1, vp1, bd1, wd1, in1, vw1, bdw1, wdw1, c2, r2, v2, vp2, bd2, wd2, in2, z3, z3c, y3s, y3cs, y3, y3c, p3, p3c,
      c3, v3, bd3, wd3, in3, c4, v4, bd4, wd4, in4, work, work2, token, ssem, rsem) = rest
     count = dict(gx=sizes[0], gy=sizes[1], gz=sizes[2])
     gx, gy, gz = lax.axis_index("gx"), lax.axis_index("gy"), lax.axis_index("gz")
@@ -702,7 +702,18 @@
     finish(halo_v2)
     halo_v2 = send_y2(lambda a, b: vp2.at[a, b])
     finish(halo_v1)
-    clean(vp1, valid1, 2, 22)
+    column1 = 64 * gx - 32 + jnp.concatenate([lane] * 4, axis=0)
+    inside1 = jnp.where(column1 >= 0, 1, 0) * jnp.where(column1 < 64 * sizes[0], 1, 0)
+    turn = lax.rem(32 + 64 * (sizes[0] - gx), 64 * sizes[0])
+
+    def beside(plane, valid):
+        return jnp.where(valid > 0, pltpu.roll(plane, turn, 1)[:, 0:128], 0.0)
+
+    for p in range(2, 22):
+        vw1[p] = beside(vp1[p], inside1 * valid1(p)[:, 0:128])
+    for p in range(3, 21):
+        bdw1[p] = beside(bd1[p], inside1)
+        wdw1[p] = beside(wd1[p], inside1)
 
     finish(right3)
     for k in range(8):
@@ -820,45 +831,45 @@
     half_sweep(vp2, bd2_at, wd2_at, 4, 16, 0, edges2, B2)
     half_sweep(vp2, bd2_at, wd2_at, 5, 15, 1, edges2, B2)
 
-    def spread(wide, rows):
-        for h in (0, 1):
-            part = wide[:, 128 * h : 128 * h + 128]
-            work2[h, pl.ds(0, rows, stride=2), :] = part
-            work2[h, pl.ds(1, rows, stride=2), :] = part
-
     def copied(base, rows):
         return jnp.concatenate([work2[h, pl.ds(base, rows), :] for h in (0, 1)], axis=1)
 
-    wide_i, wide_l = iota((128, 256), 0), iota((128, 256), 1)
-    from_second = jnp.where((wide_l >> 1) == wide_i, 1.0, 0.0).astype(F32)
+    from_second = jnp.where(((64 * gx - 32 + lane_i) >> 1) == row_i, 1.0, 0.0).astype(F32)
     picked = []
     for p in range(5, 15):
         picked += [vp2[p, 0:8], jnp.where(low4, vp2[p, 8:16], vp2[p, 16:24])]
     wide = dot(jnp.concatenate(picked, axis=0), from_second)
-    spread(wide, 160)
+    work[pl.ds(0, 160, stride=2), :] = wide
+    work[pl.ds(1, 160, stride=2), :] = wide
 
     def add1(i, carry):
-        correction = copied(32 * i, 32)
-        vp1[2 + 2 * i] = vp1[2 + 2 * i] + correction
-        vp1[3 + 2 * i] = vp1[3 + 2 * i] + correction
+        correction = work[32 * i : 32 * i + 32, :]
+        vw1[2 + 2 * i] = vw1[2 + 2 * i] + correction
+        vw1[3 + 2 * i] = vw1[3 + 2 * i] + correction
         return carry
 
     for i in range(10):
         add1(i, 0)
-    half_sweep(vp1, bd1_at, wd1_at, 3, 21, 0, edges1, B1)
-    half_sweep(vp1, bd1_at, wd1_at, 4, 20, 1, edges1, B1)
-    half_sweep(vp1, bd1_at, wd1_at, 5, 19, 0, edges1, B1)
-    half_sweep(vp1, bd1_at, wd1_at, 6, 18, 1, edges1, B1)
-
-    first_i, first_l = iota((256, 256), 0), iota((256, 256), 1)
+    bdw1_at = lambda p: bdw1[p]
+    wdw1_at = lambda p: wdw1[p]
+    no_edges = (None,) * 4
+    half_sweep(vw1, bdw1_at, wdw1_at, 3, 21, 0, no_edges, B1)
+    half_sweep(vw1, bdw1_at, wdw1_at, 4, 20, 1, no_edges, B1)
+    half_sweep(vw1, bdw1_at, wdw1_at, 5, 19, 0, no_edges, B1)
+    half_sweep(vw1, bdw1_at, wdw1_at, 6, 18, 1, no_edges, B1)
+
+    first_i, first_l = iota((128, 256), 0), iota((128, 256), 1)
     column = jnp.where(first_l < NX + 4, first_l, jnp.where(first_l >= 2 * NX - 4, first_l - 2 * NX, -1024))
-    from_first = jnp.where(((gx * NX + column) >> 1) == first_i, 1.0, 0.0).astype(F32)
-    tile_low2 = jnp.concatenate([sub, sub], axis=1) < 2
+    x = jnp.where(column > -1024, gx * NX + column, -1024)
+    from_first = jnp.where((x >> 1) == 64 * gx - 32 + first_i, 1.0, 0.0).astype(F32)
     picked = []
     for p in range(6, 18):
-        picked += [vp1[p, 0:16], jnp.where(tile_low2, vp1[p, 16:24], pltpu.roll(vp1[p, 24:32], 4, 0))]
+        picked += [vw1[p, 0:16], jnp.where(sub < 2, vw1[p, 16:24], pltpu.roll(vw1[p, 24:32], 4, 0))]
     wide = dot(jnp.concatenate(picked, axis=0), from_first)
-    spread(wide, 288)
+    for h in (0, 1):
+        part = wide[:, 128 * h : 128 * h + 128]
+        work2[h, pl.ds(0, 288, stride=2), :] = part
+        work2[h, pl.ds(1, 288, stride=2), :] = part
 
     def add0(i, carry):
         correction = copied(48 * i, 40)
@@ -920,6 +931,9 @@
         vmem(24, 32, 256),
         vmem(24, 32, 256),
         vmem(24, 32, 256),
+        vmem(24, 32, 128),
+        vmem(24, 32, 128),
+        vmem(24, 32, 128),
         vmem(2, 20, 24, 128),
         vmem(20, 24, 128),
         vmem(20, 24, 128),

time: 69.7 us -> 68.4 us (0.981)
  Pallas kernels: 67.9 us -> 66.5 us
    pallas_call x1, Pallas kernels: 67.9 us -> 66.5 us  [local(): pl.pallas_call(functools.partial(kernel, sizes), out_shape=jax.ShapeDtype...]
where the time goes in v4:
time: 68.4 us; the launch traced here: 68.2 us
  Pallas kernels  66.5 us (97%)
  local copies, waits for them, and re-layouts  1.67 us (2%)
    pallas_call x1, Pallas kernels, local(): pl.pallas_call(functools.partial(kernel, sizes), out_shape=jax.ShapeDtype...  66.5 us
    unnamed x1, local copies, waits for them, and re-layouts  1.67 us

profile of v4, /device:TPU:1, one launch (start us, length us, event | category | flops | bytes accessed | tf_op | source)
XLA Modules:
  0.0 68.2 jit_solution(9460760977261352269)
XLA Ops:
  0.0 66.5 %v_cycle.1 = f32[16,32,128]{2,1,0:T(8,128)} custom-call(f32[16,32,128]{2,1,0:T(8,128)} %refs_0_.1, s32[16,32,128]{2,1,0:T(8,128)} %refs_1_.1), custom_call_target="tpu_custom_call" | custom-call | tf_op jit(solution)/shard_map/v_cycle/pallas_call | solution.py:968
  66.5 1.7 %copy.4 = f32[16,32,128]{2,1,0:T(8,128)} copy(f32[16,32,128]{2,1,0:T(8,128)} %v_cycle.1) | data formatting | bytes 524288

commit v5 on v4

--- a/solution.py
+++ b/solution.py
@@ -562,14 +562,15 @@
     view_r1 = lambda a, b: r1.at[a, b]
     right1 = send_halo1(view_r1, view_r1, 5)
 
+    finish(coef1)
+    coefficients(lambda f, p: c1[f, p], wd1, in1, (3, 21), 0.25, valid1)
+    finish(coef2)
+    coefficients(lambda f, p: c2[f, p], wd2, in2, (2, 18), 0.0625, valid2)
+
     finish(halo_v0)
     for z in range(NZ + 8):
         tv[z] = jnp.where(low4, vp0[0, z, 0:8, 0:NX], vp0[0, z, NY - 8 : NY, 0:NX])
     halo_v0 = [send(tv, syv.at[0 if b == 1 else 1], (0, b, 0)) for b in (1, -1)]
-    finish(coef1)
-    coefficients(lambda f, p: c1[f, p], wd1, in1, (3, 21), 0.25, valid1)
-    finish(coef2)
-    coefficients(lambda f, p: c2[f, p], wd2, in2, (2, 18), 0.0625, valid2)
 
     finish(right1)
 
@@ -701,6 +702,10 @@
     fill_v0()
     finish(halo_v2)
     halo_v2 = send_y2(lambda a, b: vp2.at[a, b])
+    finish(right3)
+    for k in range(8):
+        y3s[0, k] = z3[k] + z3[k + 8]
+    right3 = gather_gy(y3s, y3)
     finish(halo_v1)
     column1 = 64 * gx - 32 + jnp.concatenate([lane] * 4, axis=0)
     inside1 = jnp.where(column1 >= 0, 1, 0) * jnp.where(column1 < 64 * sizes[0], 1, 0)
@@ -714,11 +719,6 @@
     for p in range(3, 21):
         bdw1[p] = beside(bd1[p], inside1)
         wdw1[p] = beside(wd1[p], inside1)
-
-    finish(right3)
-    for k in range(8):
-        y3s[0, k] = z3[k] + z3[k + 8]
-    right3 = gather_gy(y3s, y3)
     finish(halo_v2)
     clean(vp2, valid2, 0, 20)
     finish(right3)
@@ -959,8 +959,8 @@
         vmem(8, 16, 128),
         vmem(8, 16, 128),
         vmem(8, 16, 128),
-        vmem(640, 128),
-        vmem(2, 576, 128),
+        vmem(648, 128),
+        vmem(2, 584, 128),
         pltpu.SemaphoreType.REGULAR((2,)),
         pltpu.SemaphoreType.DMA((COPIES,)),
         pltpu.SemaphoreType.DMA((COPIES,)),

time: 68.4 us -> 68.4 us (level)
  no operation moved by 1% of the time
where the time goes in v5:
time: 68.4 us; the launch traced here: 68.2 us
  Pallas kernels  66.5 us (97%)
  local copies, waits for them, and re-layouts  1.67 us (2%)
    pallas_call x1, Pallas kernels, local(): pl.pallas_call(functools.partial(kernel, sizes), out_shape=jax.ShapeDtype...  66.5 us
    unnamed x1, local copies, waits for them, and re-layouts  1.67 us

profile of v5, /device:TPU:1, one launch (start us, length us, event | category | flops | bytes accessed | tf_op | source)
XLA Modules:
  0.0 68.2 jit_solution(1339852096402019462)
XLA Ops:
  0.0 66.5 %v_cycle.1 = f32[16,32,128]{2,1,0:T(8,128)} custom-call(f32[16,32,128]{2,1,0:T(8,128)} %refs_0_.1, s32[16,32,128]{2,1,0:T(8,128)} %refs_1_.1), custom_call_target="tpu_custom_call" | custom-call | tf_op jit(solution)/shard_map/v_cycle/pallas_call | solution.py:968
  66.5 1.7 %copy.4 = f32[16,32,128]{2,1,0:T(8,128)} copy(f32[16,32,128]{2,1,0:T(8,128)} %v_cycle.1) | data formatting | bytes 524288
